TPU v7x, 32 devices: a whole 2x2x4 slice. The times are simulated.
32 devices in a mesh: space: 8 (over z, y), chan: 4 (over x, core).
Axes of the slice: x: 2, y: 2, z: 4, core: 2. Of those that a mesh axis runs over, the one named last changes fastest.
Arguments:
- features: bfloat16 [128, 16, 512], P('chan', 'space'), may hold values from -6 to 6
- mask_packed: int32 [16, 16], P('space'), may hold values from -2147483648 to 2147483646
- neighbours: int32 [16, 26], P('space'), may hold values from 0 to 10, as said below
- send_list: int32 [8, 8, 1], P('space'), may hold values from 0 to 2, as said below
- weights: bfloat16 [27, 128, 128], P(None, 'chan'), may hold values from -0.109375 to 0.109375
- cotangent: bfloat16 [128, 16, 512], P('chan', 'space'), may hold values from -6 to 6
Outputs:
- activated: bfloat16 [128, 16, 512], P('chan', 'space')
- grad_features: bfloat16 [128, 16, 512], P('chan', 'space')
- grad_weights: float32 [27, 128, 128], P(None, 'chan')
Inputs may be any that keep to these rules, and one draw needn't show every extreme that they name: `neighbours`: entry j of a brick's row names the neighbour at the j-th of the 26 offsets as a row of its partition's table: 0 to 1 the partition's own bricks, 2 + k + s the s-th brick received from the adjacent tile in the k-th planar move, used only where the offset's planar part is that move and the tile exists, 10 none. Every slot that is named is filled in send_list. send_list[q, k, s] is the local index of the s-th brick that partition q sends to the partition whose tile lies at q's tile moved by minus the k-th planar move, or 2 where that slot is empty; a slot is filled exactly when some brick of that partition names it.
All inputs are finite; a program needn't handle non-finite values.
Results may differ from a plain program's by a relative error of at most 0.005.
Values may be sent and summed in bfloat16 or wider, within the bound.
A program may use at most 128 MiB of HBM per device.

v0:
```python
import math

import jax
import jax.numpy as jnp
from jax import lax
from jax.sharding import PartitionSpec as P

BRICK = 8
VOX = 512


all_offsets = [
    (along_x, along_y, along_z)
    for along_x in (-1, 0, 1)
    for along_y in (-1, 0, 1)
    for along_z in (-1, 0, 1)
]
tile_moves = [
    (move_a, move_b) for move_a in (-1, 0, 1) for move_b in (-1, 0, 1) if (move_a, move_b) != (0, 0)
]
tile_steps = [move_a * 4 + move_b for move_a, move_b in tile_moves]


def passed_along(shard, axis, by):
    count = lax.axis_size(axis)
    pairs = [(i, i + by) for i in range(count) if 0 <= i + by < count]
    return lax.ppermute(shard, axis, pairs)


def unpack_mask(packed):
    shifts = jnp.arange(32, dtype=jnp.int32)
    bitflags = lax.shift_right_logical(packed[:, :, None], shifts[None, None, :]) & 1
    return bitflags.reshape(packed.shape[0], packed.shape[1] * 32).astype(jnp.float32)


def side_slice(direction, extent):
    if direction == -1:
        return slice(extent - 1, extent)
    if direction == 0:
        return slice(0, extent)
    return slice(0, 1)


def cycle_slice(direction, extent):
    if direction == -1:
        return slice(0, 1)
    if direction == 0:
        return slice(1, extent + 1)
    return slice(extent + 1, extent + 2)


def neighbour_slot(along_x, along_y, along_z):
    linear = (along_x + 1) * 9 + (along_y + 1) * 3 + (along_z + 1)
    return linear if linear < 13 else linear - 1


def window_start(extent):
    padded = extent + 2
    return padded * padded + padded + 1


def flat_length(extent):
    padded = extent + 2
    needed = 2 * (padded * padded + padded + 1) + extent * padded * padded
    return (needed + 127) // 128 * 128


def assemble(source_table, center, indices, extent):
    channels, brick_count = (center.shape[0], center.shape[1])
    planes = []
    for along_x in (-1, 0, 1):
        columns = []
        for along_y in (-1, 0, 1):
            pieces = []
            for along_z in (-1, 0, 1):
                if (along_x, along_y, along_z) == (0, 0, 0):
                    source = center
                else:
                    source = jnp.take(
                        source_table, indices[:, neighbour_slot(along_x, along_y, along_z)], axis=1
                    )
                source = source.reshape(channels, brick_count, extent, extent, extent)
                pieces.append(
                    source[
                        :,
                        :,
                        side_slice(along_x, extent),
                        side_slice(along_y, extent),
                        side_slice(along_z, extent),
                    ]
                )
            columns.append(jnp.concatenate(pieces, axis=4))
        planes.append(jnp.concatenate(columns, axis=3))
    padded_cube = jnp.concatenate(planes, axis=2)
    padded_edge = extent + 2
    flattened = padded_cube.reshape(channels, brick_count, padded_edge**3)
    return jnp.pad(flattened, ((0, 0), (0, 0), (0, flat_length(extent) - padded_edge**3)))


def columns_of(padded_block, extent):
    padded = extent + 2
    anchor = window_start(extent)
    length = extent * padded * padded
    windows = []
    for along_x, along_y, along_z in all_offsets:
        offset_flat = along_x * padded * padded + along_y * padded + along_z
        windows.append(padded_block[:, :, anchor + offset_flat : anchor + offset_flat + length])
    return jnp.stack(windows, axis=0)


def interior(window, extent):
    padded = extent + 2
    leading = window.shape[:-1]
    shaped = window.reshape(leading + (extent, padded, padded))[..., :extent, :extent]
    return shaped.reshape(leading + (extent**3,))


def embed_window(values, extent):
    padded = extent + 2
    leading = values.shape[:-1]
    shaped = values.reshape(leading + (extent, extent, extent))
    widths = [(0, 0)] * len(leading) + [(0, 0), (0, padded - extent), (0, padded - extent)]
    return jnp.pad(shaped, widths).reshape(leading + (extent * padded * padded,))


def spread(products, extent, full_length, first_offset):
    padded = extent + 2
    anchor = window_start(extent)
    length = products.shape[-1]
    result = jnp.zeros(products.shape[1:-1] + (full_length,), jnp.float32)
    for position in range(products.shape[0]):
        along_x, along_y, along_z = all_offsets[first_offset + position]
        placed_at = anchor + along_x * padded * padded + along_y * padded + along_z
        result = result + jnp.pad(
            products[position], ((0, 0), (0, 0), (placed_at, full_length - placed_at - length))
        )
    return result


def scatter_block(grad_block, indices, table_rows, extent):
    channels, brick_count = (grad_block.shape[0], grad_block.shape[1])
    padded = extent + 2
    padded_cube = grad_block[:, :, : padded**3].reshape(
        channels, brick_count, padded, padded, padded
    )
    interior_span = slice(1, extent + 1)
    center = padded_cube[:, :, interior_span, interior_span, interior_span].reshape(
        channels, brick_count, extent**3
    )
    accumulated = jnp.zeros((channels, table_rows, extent, extent, extent), jnp.float32)
    for along_x, along_y, along_z in all_offsets:
        if (along_x, along_y, along_z) == (0, 0, 0):
            continue
        column = neighbour_slot(along_x, along_y, along_z)
        rim_piece = padded_cube[
            :,
            :,
            cycle_slice(along_x, extent),
            cycle_slice(along_y, extent),
            cycle_slice(along_z, extent),
        ]
        accumulated = accumulated.at[
            :,
            indices[:, column],
            side_slice(along_x, extent),
            side_slice(along_y, extent),
            side_slice(along_z, extent),
        ].add(rim_piece)
    return (center, accumulated.reshape(channels, table_rows, extent**3))


def on_device(features, mask_packed, neighbours, send_list, weights, cotangent):
    groups = lax.axis_size("space")
    chan_width = features.shape[0]
    brick_count = features.shape[1]
    total_width = weights.shape[2]
    slot_count = send_list.shape[2]
    empty_row = brick_count + 8 * slot_count
    mask_full = unpack_mask(mask_packed)
    masked = features * mask_full[None].astype(jnp.bfloat16)
    with_zero = jnp.concatenate([masked, jnp.zeros((chan_width, 1, VOX), jnp.bfloat16)], axis=1)
    send_local = send_list[0]
    arrivals = []
    for move in range(8):
        outgoing = jnp.take(with_zero, send_local[move], axis=1)
        arrivals.append(passed_along(outgoing, "space", -tile_steps[move]))
    received = jnp.concatenate(arrivals, axis=1)
    source_table = jnp.concatenate(
        [masked, received, jnp.zeros((chan_width, 1, VOX), jnp.bfloat16)], axis=1
    )
    padded_block = assemble(source_table, masked, neighbours, BRICK)
    full_length = padded_block.shape[2]
    stacked = columns_of(padded_block, BRICK).reshape(27 * chan_width, brick_count, -1)
    weight_rows = weights.reshape(27 * chan_width, total_width)
    picked = weight_rows
    summed = lax.psum_scatter(
        interior(
            jnp.einsum("rc,rbt->cbt", picked, stacked, preferred_element_type=jnp.float32), BRICK
        ),
        "chan",
        scatter_dimension=0,
        tiled=True,
    )
    pre_act = summed * mask_full[None]
    gate_value = jax.nn.sigmoid(pre_act)
    activated = (pre_act * gate_value).astype(jnp.bfloat16)
    grad_conv = (
        cotangent.astype(jnp.float32)
        * mask_full[None]
        * gate_value
        * (1.0 + pre_act * (1.0 - gate_value))
    ).astype(jnp.bfloat16)
    grad_block = jnp.zeros((chan_width, brick_count, full_length), jnp.float32)
    window = embed_window(lax.all_gather(grad_conv, "chan", axis=0, tiled=True), BRICK)
    part_weight = jnp.einsum("rbt,cbt->rc", stacked, window, preferred_element_type=jnp.float32)
    grad_weight = part_weight
    picked = weight_rows
    for group_index in range(3):
        row_block = picked[group_index * 9 * chan_width : (group_index + 1) * 9 * chan_width]
        products = jnp.einsum("rc,cbt->rbt", row_block, window, preferred_element_type=jnp.float32)
        products = products.reshape(9, chan_width, brick_count, -1)
        grad_block = grad_block + spread(products, BRICK, full_length, group_index * 9)
    grad_weight, grad_block = (grad_weight, grad_block)
    grad_scale = 1.0 / math.sqrt(brick_count * groups * VOX)
    grad_weights = (lax.psum(grad_weight, "space") * grad_scale).reshape(
        27, chan_width, total_width
    )
    center, accumulated = scatter_block(grad_block, neighbours, empty_row + 1, BRICK)
    own_total = center + accumulated[:, :brick_count]
    going_back = accumulated[:, brick_count:empty_row].astype(jnp.bfloat16)
    pieces_back = []
    for move in range(8):
        back_piece = going_back[:, move * slot_count : (move + 1) * slot_count]
        pieces_back.append(passed_along(back_piece, "space", tile_steps[move]).astype(jnp.float32))
    returned = jnp.concatenate(pieces_back, axis=1)
    return_rows = send_local.reshape(-1)
    own_padded = jnp.concatenate([own_total, jnp.zeros((chan_width, 1, VOX), jnp.float32)], axis=1)
    own_padded = own_padded.at[:, return_rows].add(returned)
    grad_features = (own_padded[:, :brick_count] * mask_full[None]).astype(jnp.bfloat16)
    return (activated, grad_features, grad_weights)


def solution(mesh):
    return jax.shard_map(
        on_device,
        mesh=mesh,
        in_specs=(
            P("chan", "space", None),
            P("space", None),
            P("space", None),
            P("space", None, None),
            P(None, "chan", None),
            P("chan", "space", None),
        ),
        out_specs=(P("chan", "space", None), P("chan", "space", None), P(None, "chan", None)),
        check_vma=False,
    )
```

profile of v0, /device:TPU:0, one launch (start us, length us, event | category | flops | bytes accessed | tf_op | source)
XLA Modules:
  0.0 712.0 jit_solution(17963421086575264553)
XLA Ops:
  22.0 5.9 collective-permute-start.2
  51.0 3.4 collective-permute-done.6
  97.3 9.6 %reduce-scatter.2.cloned.1.call-done = f32[32,2,512]{2,0,1:T(8,128)} async-done(((f32[128,2,512]{2,0,1:T(8,128)}), f32[32,2,512]{2,0,1:T(8,128)}) %reduce-scatter.2.cloned.1.call-update) | async-done | bytes 131088 | tf_op jit(solution)/shard_map/reduce_scatter | solution.py:196
  108.5 6.0 all_gather.3
  124.4 26.5 %while.27 = (s32[]{:T(128)}, f32[32,11,8,8,8]{0,4,3,2,1:T(8,128)S(1)}, s32[2,4]{1,0:T(2,128)}, f32[2,32,1,1,1]{1,4,3,2,0:T(1,128)}, s32[]{:T(128)}, /*index=5*/s32[5]{0:T(128)}, s32[1]{0:T(128)}, s32[]{:T(128)}) while((s32[]{:T(128)}, f32[32,11,8,8,8]{0,4,3,2,1:T(8,128)S(1)}, s32[2,4]{1,0:T(2,128)}, f32[2,32,1,1,1]{1,4,3,2,0:T(1,128)}, s32[]{:T(128)}, ...), condition=%wide.while_cond.1, body=%wide.while_body.1.sunk | while | flops 85 | bytes 899 | solution.py:168
  130.2 4.4 broadcast_select_fusion.36
  143.4 4.4 broadcast_select_fusion.36
  150.9 16.9 %while.28 = (s32[]{:T(128)}, f32[32,11,8,8,8]{0,4,3,2,1:T(8,128)S(1)}, s32[2,3]{1,0:T(2,128)}, f32[2,32,1,1,8]{1,0,4,3,2:T(2,128)}, s32[]{:T(128)}, /*index=5*/s32[5]{0:T(128)}, s32[1]{0:T(128)}) while((s32[]{:T(128)}, f32[32,11,8,8,8]{0,4,3,2,1:T(8,128)S(1)}, s32[2,3]{1,0:T(2,128)}, f32[2,32,1,1,8]{1,0,4,3,2:T(2,128)}, s32[]{:T(128)}, ...), condition=%wide.while_cond.2, body=%wide.while_body.2.sunk | while | flops 533 | bytes 14563 | solution.py:168
  167.8 27.3 %while.29 = (s32[]{:T(128)}, f32[32,11,8,8,8]{0,4,3,2,1:T(8,128)S(1)}, s32[2,4]{1,0:T(2,128)}, f32[2,32,1,1,1]{1,4,3,2,0:T(1,128)}, s32[]{:T(128)}, /*index=5*/s32[5]{0:T(128)}, s32[1]{0:T(128)}, s32[]{:T(128)}) while((s32[]{:T(128)}, f32[32,11,8,8,8]{0,4,3,2,1:T(8,128)S(1)}, s32[2,4]{1,0:T(2,128)}, f32[2,32,1,1,1]{1,4,3,2,0:T(1,128)}, s32[]{:T(128)}, ...), condition=%wide.while_cond.3, body=%wide.while_body.3.sunk | while | flops 85 | bytes 899 | solution.py:168
  169.2 3.3 concatenate.256
  173.8 4.4 broadcast_select_fusion.37
  178.2 3.3 dynamic-update-slice.163
  182.8 3.3 concatenate.256
  187.5 4.4 broadcast_select_fusion.37
  191.8 3.3 dynamic-update-slice.163
  195.2 23.3 %while.30 = (s32[]{:T(128)}, f32[32,11,8,8,8]{0,4,3,2,1:T(8,128)S(1)}, s32[2,3]{1,0:T(2,128)}, f32[2,32,1,8,1]{1,0,4,3,2:T(2,128)}, s32[]{:T(128)}, /*index=5*/s32[5]{0:T(128)}, s32[1]{0:T(128)}, s32[]{:T(128)}) while((s32[]{:T(128)}, f32[32,11,8,8,8]{0,4,3,2,1:T(8,128)S(1)}, s32[2,3]{1,0:T(2,128)}, f32[2,32,1,8,1]{1,0,4,3,2:T(2,128)}, s32[]{:T(128)}, ...), condition=%wide.while_cond.4, body=%wide.while_body.4.sunk | while | flops 533 | bytes 5359 | solution.py:168
  200.3 3.9 broadcast_select_fusion.38
  212.0 3.9 broadcast_select_fusion.38
  218.5 14.4 %while.31 = (s32[]{:T(128)}, f32[32,11,8,8,8]{0,4,3,2,1:T(8,128)S(1)}, s32[2,2]{1,0:T(2,128)}, f32[2,32,1,8,8]{1,0,4,3,2:T(2,128)}, s32[]{:T(128)}, /*index=5*/s32[5]{0:T(128)}, s32[1]{0:T(128)}) while((s32[]{:T(128)}, f32[32,11,8,8,8]{0,4,3,2,1:T(8,128)S(1)}, s32[2,2]{1,0:T(2,128)}, f32[2,32,1,8,8]{1,0,4,3,2:T(2,128)}, s32[]{:T(128)}, ...), condition=%wide.while_cond.5, body=%wide.while_body.5.sunk | while | flops 4117 | bytes 114895 | solution.py:168
  232.9 23.1 %while.32 = (s32[]{:T(128)}, f32[32,11,8,8,8]{0,4,3,2,1:T(8,128)S(1)}, s32[2,3]{1,0:T(2,128)}, f32[2,32,1,8,1]{1,0,4,3,2:T(2,128)}, s32[]{:T(128)}, /*index=5*/s32[5]{0:T(128)}, s32[1]{0:T(128)}, s32[]{:T(128)}) while((s32[]{:T(128)}, f32[32,11,8,8,8]{0,4,3,2,1:T(8,128)S(1)}, s32[2,3]{1,0:T(2,128)}, f32[2,32,1,8,1]{1,0,4,3,2:T(2,128)}, s32[]{:T(128)}, ...), condition=%wide.while_cond.6, body=%wide.while_body.6.sunk | while | flops 533 | bytes 5359 | solution.py:168
  238.1 3.8 broadcast_select_fusion.39
  249.6 3.8 broadcast_select_fusion.39
  256.1 26.8 %while.33 = (s32[]{:T(128)}, f32[32,11,8,8,8]{0,4,3,2,1:T(8,128)S(1)}, s32[2,4]{1,0:T(2,128)}, f32[2,32,1,1,1]{1,4,3,2,0:T(1,128)}, s32[]{:T(128)}, /*index=5*/s32[5]{0:T(128)}, s32[1]{0:T(128)}, s32[]{:T(128)}) while((s32[]{:T(128)}, f32[32,11,8,8,8]{0,4,3,2,1:T(8,128)S(1)}, s32[2,4]{1,0:T(2,128)}, f32[2,32,1,1,1]{1,4,3,2,0:T(1,128)}, s32[]{:T(128)}, ...), condition=%wide.while_cond.7, body=%wide.while_body.7.sunk | while | flops 85 | bytes 899 | solution.py:168
  257.4 3.2 concatenate.260
  261.9 4.4 broadcast_select_fusion.40
  266.3 3.2 dynamic-update-slice.167
  270.8 3.2 concatenate.260
  275.3 4.3 broadcast_select_fusion.40
  279.7 3.2 dynamic-update-slice.167
  282.9 16.8 %while.34 = (s32[]{:T(128)}, f32[32,11,8,8,8]{0,4,3,2,1:T(8,128)S(1)}, s32[2,3]{1,0:T(2,128)}, f32[2,32,1,1,8]{1,0,4,3,2:T(2,128)}, s32[]{:T(128)}, /*index=5*/s32[5]{0:T(128)}, s32[1]{0:T(128)}) while((s32[]{:T(128)}, f32[32,11,8,8,8]{0,4,3,2,1:T(8,128)S(1)}, s32[2,3]{1,0:T(2,128)}, f32[2,32,1,1,8]{1,0,4,3,2:T(2,128)}, s32[]{:T(128)}, ...), condition=%wide.while_cond.8, body=%wide.while_body.8.sunk | while | flops 533 | bytes 14563 | solution.py:168
  299.7 26.1 %while.35 = (s32[]{:T(128)}, f32[32,11,8,8,8]{0,4,3,2,1:T(8,128)S(1)}, s32[2,4]{1,0:T(2,128)}, f32[2,32,1,1,1]{1,4,3,2,0:T(1,128)}, s32[]{:T(128)}, /*index=5*/s32[5]{0:T(128)}, s32[1]{0:T(128)}, s32[]{:T(128)}) while((s32[]{:T(128)}, f32[32,11,8,8,8]{0,4,3,2,1:T(8,128)S(1)}, s32[2,4]{1,0:T(2,128)}, f32[2,32,1,1,1]{1,4,3,2,0:T(1,128)}, s32[]{:T(128)}, ...), condition=%wide.while_cond.9, body=%wide.while_body.9.sunk | while | flops 85 | bytes 899 | solution.py:168
  305.4 4.2 broadcast_select_fusion.41
  309.7 3.1 dynamic-update-slice.169
  318.5 4.1 broadcast_select_fusion.41
  325.8 22.8 %while.36 = (s32[]{:T(128)}, f32[32,11,8,8,8]{0,4,3,2,1:T(8,128)S(1)}, s32[2,3]{1,0:T(2,128)}, f32[2,32,8,1,1]{1,0,4,3,2:T(2,128)}, s32[]{:T(128)}, /*index=5*/s32[5]{0:T(128)}, s32[1]{0:T(128)}, s32[]{:T(128)}) while((s32[]{:T(128)}, f32[32,11,8,8,8]{0,4,3,2,1:T(8,128)S(1)}, s32[2,3]{1,0:T(2,128)}, f32[2,32,8,1,1]{1,0,4,3,2:T(2,128)}, s32[]{:T(128)}, ...), condition=%wide.while_cond.10, body=%wide.while_body.10.sunk | while | flops 533 | bytes 5359 | solution.py:168
  330.9 3.8 broadcast_select_fusion.42
  342.3 3.8 broadcast_select_fusion.42
  348.6 12.6 %while.37 = (s32[]{:T(128)}, f32[32,11,8,8,8]{0,4,3,2,1:T(8,128)S(1)}, s32[2,2]{1,0:T(2,128)}, f32[2,32,8,1,8]{1,0,4,3,2:T(2,128)S(1)}, s32[]{:T(128)}, /*index=5*/s32[5]{0:T(128)}, s32[1]{0:T(128)}) while((s32[]{:T(128)}, f32[32,11,8,8,8]{0,4,3,2,1:T(8,128)S(1)}, s32[2,2]{1,0:T(2,128)}, f32[2,32,8,1,8]{1,0,4,3,2:T(2,128)S(1)}, s32[]{:T(128)}, ...), condition=%wide.while_cond.11, body=%wide.while_body.11.sunk | while | flops 4117 | bytes 114895 | solution.py:168
  361.2 18.9 %while.38 = (s32[]{:T(128)}, f32[32,11,8,8,8]{0,4,3,2,1:T(8,128)S(1)}, s32[2,3]{1,0:T(2,128)}, f32[2,32,8,1,1]{1,0,4,3,2:T(2,128)}, s32[]{:T(128)}, /*index=5*/s32[5]{0:T(128)}, s32[1]{0:T(128)}, s32[]{:T(128)}) while((s32[]{:T(128)}, f32[32,11,8,8,8]{0,4,3,2,1:T(8,128)S(1)}, s32[2,3]{1,0:T(2,128)}, f32[2,32,8,1,1]{1,0,4,3,2:T(2,128)}, s32[]{:T(128)}, ...), condition=%wide.while_cond.12, body=%wide.while_body.12.sunk | while | flops 533 | bytes 5359 | solution.py:168
  380.2 14.9 %while.39 = (s32[]{:T(128)}, f32[32,11,8,8,8]{0,4,3,2,1:T(8,128)S(1)}, s32[2,2]{1,0:T(2,128)}, f32[2,32,8,8,1]{1,0,4,3,2:T(2,128)S(1)}, s32[]{:T(128)}, /*index=5*/s32[5]{0:T(128)}, s32[1]{0:T(128)}, s32[]{:T(128)}) while((s32[]{:T(128)}, f32[32,11,8,8,8]{0,4,3,2,1:T(8,128)S(1)}, s32[2,2]{1,0:T(2,128)}, f32[2,32,8,8,1]{1,0,4,3,2:T(2,128)S(1)}, ...), condition=%wide.while_cond.13, body=%wide.while_body.13.sunk | while | flops 4117 | bytes 41179 | solution.py:168
  395.2 14.9 %while.40 = (s32[]{:T(128)}, f32[32,11,8,8,8]{0,4,3,2,1:T(8,128)S(1)}, s32[2,2]{1,0:T(2,128)}, f32[2,32,8,8,1]{1,0,4,3,2:T(2,128)S(1)}, s32[]{:T(128)}, /*index=5*/s32[5]{0:T(128)}, s32[1]{0:T(128)}, s32[]{:T(128)}) while((s32[]{:T(128)}, f32[32,11,8,8,8]{0,4,3,2,1:T(8,128)S(1)}, s32[2,2]{1,0:T(2,128)}, f32[2,32,8,8,1]{1,0,4,3,2:T(2,128)S(1)}, ...), condition=%wide.while_cond.14, body=%wide.while_body.14.sunk | while | flops 4117 | bytes 41179 | solution.py:168
  410.2 19.5 %while.41 = (s32[]{:T(128)}, f32[32,11,8,8,8]{0,4,3,2,1:T(8,128)S(1)}, s32[2,3]{1,0:T(2,128)}, f32[2,32,8,1,1]{1,0,4,3,2:T(2,128)}, s32[]{:T(128)}, /*index=5*/s32[5]{0:T(128)}, s32[1]{0:T(128)}, s32[]{:T(128)}) while((s32[]{:T(128)}, f32[32,11,8,8,8]{0,4,3,2,1:T(8,128)S(1)}, s32[2,3]{1,0:T(2,128)}, f32[2,32,8,1,1]{1,0,4,3,2:T(2,128)}, s32[]{:T(128)}, ...), condition=%wide.while_cond.15, body=%wide.while_body.15.sunk | while | flops 533 | bytes 5359 | solution.py:168
  414.8 3.2 broadcast_select_fusion.46
  424.6 3.2 broadcast_select_fusion.46
  429.7 13.6 %while.42 = (s32[]{:T(128)}, f32[32,11,8,8,8]{0,4,3,2,1:T(8,128)S(1)}, s32[2,2]{1,0:T(2,128)}, f32[2,32,8,1,8]{1,0,4,3,2:T(2,128)}, s32[]{:T(128)}, /*index=5*/s32[5]{0:T(128)}, s32[1]{0:T(128)}) while((s32[]{:T(128)}, f32[32,11,8,8,8]{0,4,3,2,1:T(8,128)S(1)}, s32[2,2]{1,0:T(2,128)}, f32[2,32,8,1,8]{1,0,4,3,2:T(2,128)}, s32[]{:T(128)}, ...), condition=%wide.while_cond.16, body=%wide.while_body.16.sunk | while | flops 4117 | bytes 114895 | solution.py:168
  443.4 18.3 %while.43 = (s32[]{:T(128)}, f32[32,11,8,8,8]{0,4,3,2,1:T(8,128)S(1)}, s32[2,3]{1,0:T(2,128)}, f32[2,32,8,1,1]{1,0,4,3,2:T(2,128)S(1)}, s32[]{:T(128)}, /*index=5*/s32[5]{0:T(128)}, s32[1]{0:T(128)}, s32[]{:T(128)}) while((s32[]{:T(128)}, f32[32,11,8,8,8]{0,4,3,2,1:T(8,128)S(1)}, s32[2,3]{1,0:T(2,128)}, f32[2,32,8,1,1]{1,0,4,3,2:T(2,128)S(1)}, ...), condition=%wide.while_cond.17, body=%wide.while_body.17.sunk | while | flops 533 | bytes 5359 | solution.py:168
  461.7 19.4 %while.44 = (s32[]{:T(128)}, f32[32,11,8,8,8]{0,4,3,2,1:T(8,128)S(1)}, s32[2,4]{1,0:T(2,128)S(1)}, f32[2,32,1,1,1]{1,4,3,2,0:T(1,128)S(1)}, s32[]{:T(128)}, /*index=5*/s32[5]{0:T(128)S(1)}, s32[1]{0:T(128)}, s32[]{:T(128)}) while((s32[]{:T(128)}, f32[32,11,8,8,8]{0,4,3,2,1:T(8,128)S(1)}, s32[2,4]{1,0:T(2,128)S(1)}, ...), condition=%wide.while_cond.18, body=%wide.while_body.18.sunk | while | flops 85 | bytes 899 | solution.py:168
  465.7 3.2 broadcast_select_fusion.48
  475.4 3.2 broadcast_select_fusion.48
  481.2 11.4 %while.45 = (s32[]{:T(128)}, f32[32,11,8,8,8]{0,4,3,2,1:T(8,128)S(1)}, s32[2,3]{1,0:T(2,128)S(1)}, f32[2,32,1,1,8]{1,0,4,3,2:T(2,128)S(1)}, s32[]{:T(128)}, /*index=5*/s32[5]{0:T(128)S(1)}, s32[1]{0:T(128)}) while((s32[]{:T(128)}, f32[32,11,8,8,8]{0,4,3,2,1:T(8,128)S(1)}, s32[2,3]{1,0:T(2,128)S(1)}, f32[2,32,1,1,8]{1,0,4,3,2:T(2,128)S(1)}, ...), condition=%wide.while_cond.19, body=%wide.while_body.19.sunk | while | flops 533 | bytes 14563 | solution.py:168
  492.6 18.9 %while.46 = (s32[]{:T(128)}, f32[32,11,8,8,8]{0,4,3,2,1:T(8,128)S(1)}, s32[2,4]{1,0:T(2,128)S(1)}, f32[2,32,1,1,1]{1,4,3,2,0:T(1,128)S(1)}, s32[]{:T(128)}, /*index=5*/s32[5]{0:T(128)S(1)}, s32[1]{0:T(128)}, s32[]{:T(128)}) while((s32[]{:T(128)}, f32[32,11,8,8,8]{0,4,3,2,1:T(8,128)S(1)}, s32[2,4]{1,0:T(2,128)S(1)}, ...), condition=%wide.while_cond.20, body=%wide.while_body.20.sunk | while | flops 85 | bytes 899 | solution.py:168
  511.6 15.6 %while.47 = (s32[]{:T(128)}, f32[32,11,8,8,8]{0,4,3,2,1:T(8,128)S(1)}, s32[2,3]{1,0:T(2,128)S(1)}, f32[2,32,1,8,1]{1,0,4,3,2:T(2,128)S(1)}, s32[]{:T(128)}, /*index=5*/s32[5]{0:T(128)S(1)}, s32[1]{0:T(128)}, s32[]{:T(128)}) while((s32[]{:T(128)}, f32[32,11,8,8,8]{0,4,3,2,1:T(8,128)S(1)}, s32[2,3]{1,0:T(2,128)S(1)}, ...), condition=%wide.while_cond.21, body=%wide.while_body.21.sunk | while | flops 533 | bytes 5359 | solution.py:168
  527.1 11.9 %while.48 = (s32[]{:T(128)}, f32[32,11,8,8,8]{0,4,3,2,1:T(8,128)S(1)}, s32[2,2]{1,0:T(2,128)}, f32[2,32,1,8,8]{1,0,4,3,2:T(2,128)S(1)}, s32[]{:T(128)}, /*index=5*/s32[5]{0:T(128)}, s32[1]{0:T(128)}) while((s32[]{:T(128)}, f32[32,11,8,8,8]{0,4,3,2,1:T(8,128)S(1)}, s32[2,2]{1,0:T(2,128)}, f32[2,32,1,8,8]{1,0,4,3,2:T(2,128)S(1)}, s32[]{:T(128)}, ...), condition=%wide.while_cond.22, body=%wide.while_body.22.sunk | while | flops 4117 | bytes 114895 | solution.py:168
  539.1 15.6 %while.49 = (s32[]{:T(128)}, f32[32,11,8,8,8]{0,4,3,2,1:T(8,128)S(1)}, s32[2,3]{1,0:T(2,128)S(1)}, f32[2,32,1,8,1]{1,0,4,3,2:T(2,128)S(1)}, s32[]{:T(128)}, /*index=5*/s32[5]{0:T(128)S(1)}, s32[1]{0:T(128)}, s32[]{:T(128)}) while((s32[]{:T(128)}, f32[32,11,8,8,8]{0,4,3,2,1:T(8,128)S(1)}, s32[2,3]{1,0:T(2,128)S(1)}, ...), condition=%wide.while_cond.23, body=%wide.while_body.23.sunk | while | flops 533 | bytes 5359 | solution.py:168
  554.7 19.8 %while.50 = (s32[]{:T(128)}, f32[32,11,8,8,8]{0,4,3,2,1:T(8,128)S(1)}, s32[2,4]{1,0:T(2,128)S(1)}, f32[2,32,1,1,1]{1,4,3,2,0:T(1,128)S(1)}, s32[]{:T(128)}, /*index=5*/s32[5]{0:T(128)S(1)}, s32[1]{0:T(128)}, s32[]{:T(128)}) while((s32[]{:T(128)}, f32[32,11,8,8,8]{0,4,3,2,1:T(8,128)S(1)}, s32[2,4]{1,0:T(2,128)S(1)}, ...), condition=%wide.while_cond.24, body=%wide.while_body.24.sunk | while | flops 85 | bytes 899 | solution.py:168
  558.8 3.2 broadcast_select_fusion.52
  568.6 3.2 broadcast_select_fusion.52
  574.5 11.7 %while.51 = (s32[]{:T(128)}, f32[32,11,8,8,8]{0,4,3,2,1:T(8,128)S(1)}, s32[2,3]{1,0:T(2,128)S(1)}, f32[2,32,1,1,8]{1,0,4,3,2:T(2,128)S(1)}, s32[]{:T(128)}, /*index=5*/s32[5]{0:T(128)S(1)}, s32[1]{0:T(128)}) while((s32[]{:T(128)}, f32[32,11,8,8,8]{0,4,3,2,1:T(8,128)S(1)}, s32[2,3]{1,0:T(2,128)S(1)}, f32[2,32,1,1,8]{1,0,4,3,2:T(2,128)S(1)}, ...), condition=%wide.while_cond.25, body=%wide.while_body.25.sunk | while | flops 533 | bytes 14563 | solution.py:168
  586.3 19.5 %while.52 = (s32[]{:T(128)}, f32[32,11,8,8,8]{0,4,3,2,1:T(8,128)S(1)}, s32[2,4]{1,0:T(2,128)S(1)}, f32[2,32,1,1,1]{1,4,3,2,0:T(1,128)S(1)}, s32[]{:T(128)}, /*index=5*/s32[5]{0:T(128)S(1)}, s32[1]{0:T(128)}, s32[]{:T(128)}) while((s32[]{:T(128)}, f32[32,11,8,8,8]{0,4,3,2,1:T(8,128)S(1)}, s32[2,4]{1,0:T(2,128)S(1)}, ...), condition=%wide.while_cond.26, body=%wide.while_body.26.sunk | while | flops 85 | bytes 899 | solution.py:168
  590.3 3.2 broadcast_select_fusion.53
  600.0 3.2 broadcast_select_fusion.53
  612.6 5.2 collective-permute-start.12
  617.8 4.7 collective-permute-done.8
  648.8 54.6 %all-reduce.45.cloned.1.call-done = f32[864,128]{1,0:T(8,128)} async-done(((f32[864,128]{1,0:T(8,128)}), f32[864,128]{1,0:T(8,128)}) %all-reduce.45.cloned.1.call-update) | async-done | bytes 442384 | tf_op jit(solution)/shard_map/psum | solution.py:225
  (664 shorter events, 477.9 us)
Async XLA Ops:
  7.2 99.8 %reduce-scatter.2.cloned.1.call-start = ((), (), s32[]{:S(2)}) async-start(), calls=%async_computation.1 | async-start | bytes 655360 | tf_op jit(solution)/shard_map/reduce_scatter | solution.py:196
  21.0 85.9 %copy-start.13 = (f32[2,512]{1,0:T(2,128)}, f32[2,512]{1,0:T(2,128)S(1)}, u32[]{:S(2)}) copy-start(f32[2,512]{1,0:T(2,128)S(1)} %get-tuple-element.678) | copy-start | bytes 12292
  22.0 25.0 %collective-permute-start.2 = (bf16[32,1,512]{2,0,1:T(8,128)(2,1)S(1)}, bf16[32,1,512]{2,0,1:T(8,128)(2,1)S(1)}, u32[]{:S(2)}, u32[]{:S(2)}) collective-permute-start(bf16[32,1,512]{2,0,1:T(8,128)(2,1)S(1)} %get-tuple-element.826), channel_id=1, source_target_pairs={{0,12},{4,16},{8,20},{12,24},{16,28},{1,13},{5,17},{9,21},{13,25},... | collective-permute-start | bytes 98312 | tf_op jit(solution)/shard_map/ppermute | solution.py:27
  31.7 12.7 %collective-permute-start = (bf16[32,1,512]{2,0,1:T(8,128)(2,1)S(1)}, bf16[32,1,512]{2,0,1:T(8,128)(2,1)S(1)}, u32[]{:S(2)}, u32[]{:S(2)}) collective-permute-start(bf16[32,1,512]{2,0,1:T(8,128)(2,1)S(1)} %get-tuple-element.832), channel_id=1, source_target_pairs={{0,20},{4,24},{8,28},{1,21},{5,25},{9,29},{2,22},{6,26},{10,30},{3... | collective-permute-start | bytes 98312 | tf_op jit(solution)/shard_map/ppermute | solution.py:27
  34.0 11.7 %collective-permute-start.1 = (bf16[32,1,512]{2,0,1:T(8,128)(2,1)S(1)}, bf16[32,1,512]{2,0,1:T(8,128)(2,1)S(1)}, u32[]{:S(2)}, u32[]{:S(2)}) collective-permute-start(bf16[32,1,512]{2,0,1:T(8,128)(2,1)S(1)} %get-tuple-element.831), channel_id=1, source_target_pairs={{0,16},{4,20},{8,24},{12,28},{1,17},{5,21},{9,25},{13,29},{2,18},{... | collective-permute-start | bytes 98312 | tf_op jit(solution)/shard_map/ppermute | solution.py:27
  36.8 11.4 %collective-permute-start.3 = (bf16[32,1,512]{2,0,1:T(8,128)(2,1)S(1)}, bf16[32,1,512]{2,0,1:T(8,128)(2,1)S(1)}, u32[]{:S(2)}, u32[]{:S(2)}) collective-permute-start(bf16[32,1,512]{2,0,1:T(8,128)(2,1)S(1)} %get-tuple-element.827), channel_id=1, source_target_pairs={{0,4},{4,8},{8,12},{12,16},{16,20},{20,24},{24,28},{1,5},{5,9},{9,... | collective-permute-start | bytes 98312 | tf_op jit(solution)/shard_map/ppermute | solution.py:27
  38.7 9.6 %collective-permute-start.4 = (bf16[32,1,512]{2,0,1:T(8,128)(2,1)S(1)}, bf16[32,1,512]{2,0,1:T(8,128)(2,1)S(1)}, u32[]{:S(2)}, u32[]{:S(2)}) collective-permute-start(bf16[32,1,512]{2,0,1:T(8,128)(2,1)S(1)} %get-tuple-element.828), channel_id=1, source_target_pairs={{4,0},{8,4},{12,8},{16,12},{20,16},{24,20},{28,24},{5,1},{9,5},{13... | collective-permute-start | bytes 98312 | tf_op jit(solution)/shard_map/ppermute | solution.py:27
  44.3 6.7 collective-permute-start.5
  45.6 8.8 %collective-permute-start.6 = (bf16[32,1,512]{2,0,1:T(8,128)(2,1)S(1)}, bf16[32,1,512]{2,0,1:T(8,128)(2,1)S(1)}, u32[]{:S(2)}, u32[]{:S(2)}) collective-permute-start(bf16[32,1,512]{2,0,1:T(8,128)(2,1)S(1)} %get-tuple-element.830), channel_id=1, source_target_pairs={{16,0},{20,4},{24,8},{28,12},{17,1},{21,5},{25,9},{29,13},{18,2},{... | collective-permute-start | bytes 98312 | tf_op jit(solution)/shard_map/ppermute | solution.py:27
  47.0 9.7 %collective-permute-start.7 = (bf16[32,1,512]{2,0,1:T(8,128)(2,1)S(1)}, bf16[32,1,512]{2,0,1:T(8,128)(2,1)S(1)}, u32[]{:S(2)}, u32[]{:S(2)}) collective-permute-start(bf16[32,1,512]{2,0,1:T(8,128)(2,1)S(1)} %get-tuple-element.825), channel_id=1, source_target_pairs={{20,0},{24,4},{28,8},{21,1},{25,5},{29,9},{22,2},{26,6},{30,10},{2... | collective-permute-start | bytes 98312 | tf_op jit(solution)/shard_map/ppermute | solution.py:27
  80.7 2.8 copy-start.3
  83.5 1.6 copy-start.20
  85.2 1.8 copy-start.1
  85.2 21.8 %copy-start.12 = (bf16[32,2,512]{2,1,0:T(2,128)(2,1)S(1)}, bf16[32,2,512]{2,1,0:T(2,128)(2,1)}, u32[]{:S(2)}) copy-start(bf16[32,2,512]{2,1,0:T(2,128)(2,1)} %param.15) | copy-start | bytes 196612
  86.9 616.4 %all-reduce.45.cloned.1.call-start = ((), (), s32[]{:S(2)}) async-start(), calls=%async_computation.2 | async-start | bytes 884736 | tf_op jit(solution)/shard_map/psum | solution.py:225
  120.1 3.9 copy-start
  361.2 82.2 %copy-start.11 = (f32[2,32,8,1,1]{1,0,4,3,2:T(2,128)S(1)}, f32[2,32,8,1,1]{1,0,4,3,2:T(2,128)}, u32[]{:S(2)}) copy-start(f32[2,32,8,1,1]{1,0,4,3,2:T(2,128)} %get-tuple-element.2123) | copy-start | bytes 6148
  361.2 100.5 %copy-start.19 = (f32[32,2,1,1,1]{0,1,4,3,2:T(2,128)S(1)}, f32[32,2,1,1,1]{0,1,4,3,2:T(2,128)}, u32[]{:S(2)}) copy-start(f32[32,2,1,1,1]{0,1,4,3,2:T(2,128)} %get-tuple-element.797) | copy-start | bytes 772
  361.2 120.0 %copy-start.8 = (f32[2,32,1,1,8]{1,0,4,3,2:T(2,128)S(1)}, f32[2,32,1,1,8]{1,0,4,3,2:T(2,128)}, u32[]{:S(2)}) copy-start(f32[2,32,1,1,8]{1,0,4,3,2:T(2,128)} %get-tuple-element.2171) | copy-start | bytes 6148
  361.2 131.4 %copy-start.18 = (f32[32,2,1,1,1]{0,1,4,3,2:T(2,128)S(1)}, f32[32,2,1,1,1]{0,1,4,3,2:T(2,128)}, u32[]{:S(2)}) copy-start(f32[32,2,1,1,1]{0,1,4,3,2:T(2,128)} %get-tuple-element.796) | copy-start | bytes 772
  361.2 150.3 %copy-start.10 = (f32[2,32,1,8,1]{1,0,4,3,2:T(2,128)S(1)}, f32[2,32,1,8,1]{1,0,4,3,2:T(2,128)}, u32[]{:S(2)}) copy-start(f32[2,32,1,8,1]{1,0,4,3,2:T(2,128)} %get-tuple-element.2216) | copy-start | bytes 6148
  395.1 66.6 %copy-start.24 = (s32[2,4]{1,0:T(2,128)S(1)}, s32[2,4]{1,0:T(2,128)}, u32[]{:S(2)}) copy-start(s32[2,4]{1,0:T(2,128)} %get-tuple-element.2146) | copy-start | bytes 100
  395.1 66.6 %copy-start.31 = (s32[5]{0:T(128)S(1)}, s32[5]{0:T(128)}, u32[]{:S(2)}) copy-start(s32[5]{0:T(128)} %get-tuple-element.2386) | copy-start | bytes 64
  395.1 86.1 %copy-start.29 = (s32[2,3]{1,0:T(2,128)S(1)}, s32[2,3]{1,0:T(2,128)}, u32[]{:S(2)}) copy-start(s32[2,3]{1,0:T(2,128)} %get-tuple-element.2170) | copy-start | bytes 76
  395.1 86.1 %copy-start.32 = (s32[5]{0:T(128)S(1)}, s32[5]{0:T(128)}, u32[]{:S(2)}) copy-start(s32[5]{0:T(128)} %get-tuple-element.2391) | copy-start | bytes 64
  395.1 97.5 %copy-start.27 = (s32[2,4]{1,0:T(2,128)S(1)}, s32[2,4]{1,0:T(2,128)}, u32[]{:S(2)}) copy-start(s32[2,4]{1,0:T(2,128)} %get-tuple-element.2191) | copy-start | bytes 100
  395.1 116.4 %copy-start.28 = (s32[2,3]{1,0:T(2,128)S(1)}, s32[2,3]{1,0:T(2,128)}, u32[]{:S(2)}) copy-start(s32[2,3]{1,0:T(2,128)} %get-tuple-element.2215) | copy-start | bytes 76
  395.2 116.4 %copy-start.33 = (s32[5]{0:T(128)S(1)}, s32[5]{0:T(128)}, u32[]{:S(2)}) copy-start(s32[5]{0:T(128)} %get-tuple-element.2394) | copy-start | bytes 64
  395.2 143.9 %copy-start.9 = (f32[2,32,1,8,1]{1,0,4,3,2:T(2,128)S(1)}, f32[2,32,1,8,1]{1,0,4,3,2:T(2,128)}, u32[]{:S(2)}) copy-start(f32[2,32,1,8,1]{1,0,4,3,2:T(2,128)} %get-tuple-element.2261) | copy-start | bytes 6148
  395.2 143.9 %copy-start.26 = (s32[2,3]{1,0:T(2,128)S(1)}, s32[2,3]{1,0:T(2,128)}, u32[]{:S(2)}) copy-start(s32[2,3]{1,0:T(2,128)} %concatenate.169) | copy-start | bytes 76
  395.2 159.5 %copy-start.17 = (f32[32,2,1,1,1]{0,1,4,3,2:T(2,128)S(1)}, f32[32,2,1,1,1]{0,1,4,3,2:T(2,128)}, u32[]{:S(2)}) copy-start(f32[32,2,1,1,1]{0,1,4,3,2:T(2,128)} %get-tuple-element.795) | copy-start | bytes 772
  395.2 159.5 %copy-start.23 = (s32[2,4]{1,0:T(2,128)S(1)}, s32[2,4]{1,0:T(2,128)}, u32[]{:S(2)}) copy-start(s32[2,4]{1,0:T(2,128)} %get-tuple-element.2284) | copy-start | bytes 100
  410.1 164.4 %copy-start.7 = (f32[2,32,1,1,8]{1,0,4,3,2:T(2,128)S(1)}, f32[2,32,1,1,8]{1,0,4,3,2:T(2,128)}, u32[]{:S(2)}) copy-start(f32[2,32,1,1,8]{1,0,4,3,2:T(2,128)} %get-tuple-element.2309) | copy-start | bytes 6148
  410.1 164.4 %copy-start.25 = (s32[2,3]{1,0:T(2,128)S(1)}, s32[2,3]{1,0:T(2,128)}, u32[]{:S(2)}) copy-start(s32[2,3]{1,0:T(2,128)} %concatenate.171) | copy-start | bytes 76
  410.2 176.1 %copy-start.16 = (f32[32,2,1,1,1]{0,1,4,3,2:T(2,128)S(1)}, f32[32,2,1,1,1]{0,1,4,3,2:T(2,128)}, u32[]{:S(2)}) copy-start(f32[32,2,1,1,1]{0,1,4,3,2:T(2,128)} %get-tuple-element.794) | copy-start | bytes 772
  410.2 176.1 %copy-start.22 = (s32[2,4]{1,0:T(2,128)S(1)}, s32[2,4]{1,0:T(2,128)}, u32[]{:S(2)}) copy-start(s32[2,4]{1,0:T(2,128)} %get-tuple-element.2329) | copy-start | bytes 100
  605.8 5.0 copy-start.15
  605.8 24.0 %copy-start.21 = (bf16[27,32,2,800]{3,1,0,2:T(8,128)(2,1)S(1)}, bf16[27,32,2,800]{3,1,0,2:T(8,128)(2,1)}, u32[]{:S(2)}) copy-start(bf16[27,32,2,800]{3,1,0,2:T(8,128)(2,1)} %copy-done.20) | copy-start | bytes 8294404
  606.8 15.7 %collective-permute-start.8 = (bf16[32,1,512]{0,2,1:T(8,128)(2,1)S(1)}, bf16[32,1,512]{0,2,1:T(8,128)(2,1)S(1)}, u32[]{:S(2)}, u32[]{:S(2)}) collective-permute-start(bf16[32,1,512]{0,2,1:T(8,128)(2,1)S(1)} %get-tuple-element.793), channel_id=1, source_target_pairs={{20,0},{24,4},{28,8},{21,1},{25,5},{29,9},{22,2},{26,6},{30,10},{2... | collective-permute-start | bytes 98312 | tf_op jit(solution)/shard_map/ppermute | solution.py:27
  608.2 17.5 %collective-permute-start.9 = (bf16[32,1,512]{0,2,1:T(8,128)(2,1)S(1)}, bf16[32,1,512]{0,2,1:T(8,128)(2,1)S(1)}, u32[]{:S(2)}, u32[]{:S(2)}) collective-permute-start(bf16[32,1,512]{0,2,1:T(8,128)(2,1)S(1)} %get-tuple-element.792), channel_id=1, source_target_pairs={{16,0},{20,4},{24,8},{28,12},{17,1},{21,5},{25,9},{29,13},{18,2},{... | collective-permute-start | bytes 98312 | tf_op jit(solution)/shard_map/ppermute | solution.py:27
  609.5 18.3 %collective-permute-start.10 = (bf16[32,1,512]{0,2,1:T(8,128)(2,1)S(1)}, bf16[32,1,512]{0,2,1:T(8,128)(2,1)S(1)}, u32[]{:S(2)}, u32[]{:S(2)}) collective-permute-start(bf16[32,1,512]{0,2,1:T(8,128)(2,1)S(1)} %get-tuple-element.791), channel_id=1, source_target_pairs={{12,0},{16,4},{20,8},{24,12},{28,16},{13,1},{17,5},{21,9},{25,13},... | collective-permute-start | bytes 98312 | tf_op jit(solution)/shard_map/ppermute | solution.py:27
  611.4 29.2 %collective-permute-start.11 = (bf16[32,1,512]{0,2,1:T(8,128)(2,1)}, bf16[32,1,512]{0,2,1:T(8,128)(2,1)}, u32[]{:S(2)}, u32[]{:S(2)}) collective-permute-start(bf16[32,1,512]{0,2,1:T(8,128)(2,1)} %get-tuple-element.790), channel_id=1, source_target_pairs={{4,0},{8,4},{12,8},{16,12},{20,16},{24,20},{28,24},{5,1},{9,5},{13... | collective-permute-start | bytes 98312 | tf_op jit(solution)/shard_map/ppermute | solution.py:27
  612.6 29.0 %collective-permute-start.12 = (bf16[32,1,512]{0,2,1:T(8,128)(2,1)}, bf16[32,1,512]{0,2,1:T(8,128)(2,1)}, u32[]{:S(2)}, u32[]{:S(2)}) collective-permute-start(bf16[32,1,512]{0,2,1:T(8,128)(2,1)} %get-tuple-element.789), channel_id=1, source_target_pairs={{0,4},{4,8},{8,12},{12,16},{16,20},{20,24},{24,28},{1,5},{5,9},{9,... | collective-permute-start | bytes 98312 | tf_op jit(solution)/shard_map/ppermute | solution.py:27
  622.6 7.2 %copy-start.4 = (bf16[32,1,512]{0,2,1:T(8,128)(2,1)}, bf16[32,1,512]{0,2,1:T(8,128)(2,1)S(1)}, u32[]{:S(2)}) copy-start(bf16[32,1,512]{0,2,1:T(8,128)(2,1)S(1)} %collective-permute-done.8) | copy-start | bytes 98308
  622.6 20.1 %collective-permute-start.13 = (bf16[32,1,512]{0,2,1:T(8,128)(2,1)}, bf16[32,1,512]{0,2,1:T(8,128)(2,1)}, u32[]{:S(2)}, u32[]{:S(2)}) collective-permute-start(bf16[32,1,512]{0,2,1:T(8,128)(2,1)} %get-tuple-element.788), channel_id=1, source_target_pairs={{0,12},{4,16},{8,20},{12,24},{16,28},{1,13},{5,17},{9,21},{13,25},... | collective-permute-start | bytes 98312 | tf_op jit(solution)/shard_map/ppermute | solution.py:27
  625.7 4.0 copy-start.5
  625.7 18.0 %collective-permute-start.14 = (bf16[32,1,512]{0,2,1:T(8,128)(2,1)S(1)}, bf16[32,1,512]{0,2,1:T(8,128)(2,1)}, u32[]{:S(2)}, u32[]{:S(2)}) collective-permute-start(bf16[32,1,512]{0,2,1:T(8,128)(2,1)S(1)} %get-tuple-element.787), channel_id=1, source_target_pairs={{0,16},{4,20},{8,24},{12,28},{1,17},{5,21},{9,25},{13,29},{2,18},{... | collective-permute-start | bytes 98312 | tf_op jit(solution)/shard_map/ppermute | solution.py:27
  627.8 1.9 copy-start.6
  627.8 16.9 %collective-permute-start.15 = (bf16[32,1,512]{0,2,1:T(8,128)(2,1)S(1)}, bf16[32,1,512]{0,2,1:T(8,128)(2,1)}, u32[]{:S(2)}, u32[]{:S(2)}) collective-permute-start(bf16[32,1,512]{0,2,1:T(8,128)(2,1)S(1)} %get-tuple-element.786), channel_id=1, source_target_pairs={{0,20},{4,24},{8,28},{1,21},{5,25},{9,29},{2,22},{6,26},{10,30},{3... | collective-permute-start | bytes 98312 | tf_op jit(solution)/shard_map/ppermute | solution.py:27
  631.5 5.3 copy-start.2
  635.5 11.5 %copy-start.30 = (s32[8]{0:T(128)S(1)}, s32[8]{0:T(128)}, u32[]{:S(2)}) copy-start(s32[8]{0:T(128)} %fusion.53) | copy-start | bytes 100
  637.5 10.6 %copy-start.14 = (f32[2,512]{1,0:T(2,128)S(1)}, f32[2,512]{1,0:T(2,128)}, u32[]{:S(2)}) copy-start(f32[2,512]{1,0:T(2,128)} %copy-done.13) | copy-start | bytes 12292
Sparse Core Ops, SparseCore 0:
  87.0 19.8 reduce-scatter.1
  633.5 69.7 all-reduce.44
where the time goes:
time: 720 us; the launch traced here: 712 us
  local copies, waits for them, and re-layouts  328 us (46%)
  other arithmetic  229 us (32%)
  waiting for transfers between devices  78.5 us (11%)
  starting transfers between devices  34.6 us (5%)
  between operations  31.2 us (4%)
    scatter-add x208, local copies, waits for them, and re-layouts  267 us
    scatter-add x104, other arithmetic  212 us
    psum x1, waiting for transfers between devices, on_device(): lax.psum(grad_weight, 'space') * grad_scale  54.6 us
    ppermute x16, starting transfers between devices, passed_along(): return lax.ppermute(shard, axis, pairs)  34.5 us
  transfers between devices with their start and end apart: 18, of which 7 were waited for; matrix products, arithmetic and copies ran while one was open for 5% of the time, Pallas kernels for 0%

commit v1 on v0

v1 whole, which is shorter than its diff:
```python
import functools
import math

import jax
import jax.numpy as jnp
from jax import lax
from jax.experimental import pallas as pl
from jax.experimental.pallas import tpu as pltpu
from jax.sharding import PartitionSpec as P

BRICK = 8
VOX = 512
LANES = 128
TILES = VOX // LANES
PLANES = BRICK + 2
MESH = pl.DeviceIdType.MESH

tile_moves = [(a, b) for a in (-1, 0, 1) for b in (-1, 0, 1) if (a, b) != (0, 0)]
tile_steps = [a * 4 + b for a, b in tile_moves]
plane_offsets = [(y, z) for y in (-1, 0, 1) for z in (-1, 0, 1)]


def neighbour_slot(along_x, along_y, along_z):
    linear = (along_x + 1) * 9 + (along_y + 1) * 3 + (along_z + 1)
    return linear if linear < 13 else linear - 1


def tile_of(along_x):
    return TILES - 1 if along_x == -1 else 0


def plan_chunks(rows, groups):
    chunk = -(-rows // groups)
    chunk = -(-chunk // 16) * 16
    return chunk, -(-rows // chunk)


def nt_dot(left, right):
    return lax.dot_general(
        left, right, (((1,), (1,)), ((), ())), preferred_element_type=jnp.float32
    )


def nn_dot(left, right):
    return jnp.dot(left, right, preferred_element_type=jnp.float32)


def kernel(
    groups, parts, width, bricks, scale,
    packed, near, sends, feat, w, cot,
    act, grad_feat, grad_w,
    table, outbox, place, expand, w_turned, w_wide, padded, stacked, comp, sum_in, gates,
    window, prod, backbox, back_in, gw_own, gw_send, gw_in, gw_all,
    halo_s, halo_r, back_s, back_r, sum_s, sum_r, gate_s, gate_r, red_s, red_r, all_s, all_r,
):
    me, mine = lax.axis_index("space"), lax.axis_index("chan")
    total = parts * width
    rows_w = 27 * width
    chunk, owners = plan_chunks(rows_w, groups)
    wide = BRICK * LANES
    cube = PLANES * LANES
    f32, bf16 = jnp.float32, jnp.bfloat16

    barrier = pltpu.get_barrier_semaphore()
    for d in range(1, groups):
        pl.semaphore_signal(
            barrier, inc=1, device_id=(lax.rem(me + d, groups), mine), device_id_type=MESH
        )
    for e in range(1, parts):
        pl.semaphore_signal(
            barrier, inc=1, device_id=(me, lax.rem(mine + e, parts)), device_id_type=MESH
        )

    lane = lax.broadcasted_iota(jnp.int32, (1, VOX), 1)
    masks = []
    for b in range(bricks):
        word = jnp.zeros((1, VOX), jnp.int32)
        for i in range(VOX // 32):
            word = jnp.where((lane >> 5) == i, packed[b, i], word)
        masks.append((lax.shift_right_logical(word, lane & 31) & 1).astype(f32))

    masked = [
        feat[:, b * VOX : (b + 1) * VOX].astype(f32) * masks[b] for b in range(bricks)
    ]
    for b in range(bricks):
        for t in range(TILES):
            table[b, t] = masked[b][:, t * LANES : (t + 1) * LANES].astype(bf16)
    table[bricks + 8] = jnp.zeros((TILES, width, LANES), bf16)
    for k, (a, _) in enumerate(tile_moves):
        chosen = jnp.full((width, LANES), sends[0, k, 0], jnp.int32)
        for t in range(TILES) if a == 0 else (tile_of(a),):
            value = jnp.zeros((width, LANES), f32)
            for b in range(bricks):
                value = jnp.where(chosen == b, masked[b][:, t * LANES : (t + 1) * LANES], value)
            outbox[k, t] = value.astype(bf16)

    pl.semaphore_wait(barrier, groups - 1 + parts - 1)

    tile_a, tile_b = me // 4, lax.rem(me, 4)

    def inside(a, b):
        return (
            (tile_a + a >= 0) & (tile_a + a < groups // 4) & (tile_b + b >= 0) & (tile_b + b < 4)
        )

    def halo(k, box, rows, base, send, recv, sign):
        a, _ = tile_moves[k]
        if a == 0:
            source, target = box.at[k], rows.at[base + k]
        else:
            source, target = box.at[k, tile_of(a)], rows.at[base + k, tile_of(a)]
        peer = jnp.clip(me + sign * tile_steps[k], 0, groups - 1)
        return pltpu.make_async_remote_copy(
            src_ref=source, dst_ref=target, send_sem=send.at[k], recv_sem=recv.at[k],
            device_id=(peer, mine), device_id_type=MESH,
        )

    forth = [halo(k, outbox, table, bricks, halo_s, halo_r, -1) for k in range(8)]
    back = [halo(k, backbox, back_in, 0, back_s, back_r, 1) for k in range(8)]
    ahead = [inside(a, b) for a, b in tile_moves]
    behind = [inside(-a, -b) for a, b in tile_moves]

    def start_if(flag, copy):
        @pl.when(flag)
        def _():
            copy.start()

    def sent_if(flag, copy):
        @pl.when(flag)
        def _():
            copy.wait_send()

    def arrived_if(flag, copy):
        @pl.when(flag)
        def _():
            copy.wait_recv()

    for k in range(8):
        start_if(behind[k], forth[k])

    row = lax.broadcasted_iota(jnp.int32, (LANES, 2 * LANES), 0)
    col = lax.broadcasted_iota(jnp.int32, (LANES, 2 * LANES), 1)
    half, at_y, at_z = row >> 6, (row >> 3) & 7, row & 7
    goal = half * LANES + (at_y + 1) * PLANES + (at_z + 1)
    side_y = {-1: at_y == BRICK - 1, 1: at_y == 0}
    side_z = {-1: at_z == BRICK - 1, 1: at_z == 0}
    for n, (y, z) in enumerate(plane_offsets):
        hit = col == goal + (BRICK * PLANES * y + BRICK * z)
        if y != 0:
            hit = hit & side_y[y]
        if z != 0:
            hit = hit & side_z[z]
        place[n] = jnp.where(hit, 1.0, 0.0).astype(bf16)
    expand[...] = jnp.where(col == goal - (PLANES + 1), 1.0, 0.0).astype(bf16)

    rows_k = w_turned.shape[1]
    for c in range(rows_k // LANES):
        have = min(rows_w - c * LANES, LANES)
        block = w[c * LANES : c * LANES + have, :].astype(f32)
        if have < LANES:
            block = jnp.concatenate([block, jnp.zeros((LANES - have, total), f32)], axis=0)
        w_turned[:, c * LANES : (c + 1) * LANES] = block.T.astype(bf16)
    for n in range(9):
        for u in range(3):
            w_wide[n * width : (n + 1) * width, u * total : (u + 1) * total] = w[
                (u * 9 + n) * width : (u * 9 + n + 1) * width, :
            ]
    if rows_k > rows_w:
        stacked[rows_w:, :] = jnp.zeros((rows_k - rows_w, bricks * wide), bf16)
    for u in range(3):
        for b in range(bricks):
            for px in range(PLANES):
                if not u <= px < u + BRICK:
                    window[
                        u * total : (u + 1) * total,
                        b * cube + px * LANES : b * cube + (px + 1) * LANES,
                    ] = jnp.zeros((total, LANES), bf16)

    for k in range(8):
        arrived_if(ahead[k], forth[k])

    built = jnp.zeros((bricks * (TILES + 2) * width, 2 * LANES), f32)
    for n, (y, z) in enumerate(plane_offsets):
        pieces = []
        for b in range(bricks):
            source = b if (y, z) == (0, 0) else near[b, neighbour_slot(0, y, z)]
            pieces.append(table[source].reshape(TILES * width, LANES))
        for x in (-1, 1):
            for b in range(bricks):
                pieces.append(table[near[b, neighbour_slot(x, y, z)], tile_of(x)])
        built = built + nn_dot(jnp.concatenate(pieces, axis=0), place[n])
    ends = bricks * TILES * width
    for b in range(bricks):
        base = b * cube
        low = ends + b * width
        high = ends + (bricks + b) * width
        padded[:, base : base + LANES] = built[low : low + width, LANES:]
        padded[:, base + cube - LANES : base + cube] = built[high : high + width, :LANES]
        for t in range(TILES):
            at = (b * TILES + t) * width
            padded[:, base + (2 * t + 1) * LANES : base + (2 * t + 3) * LANES] = built[
                at : at + width, :
            ]

    length = bricks * cube
    shifts = [(y + 1) * PLANES + (z + 1) for y, z in plane_offsets]
    for n in range(9):
        value = padded[...]
        if shifts[n]:
            value = pltpu.roll(value, length - shifts[n], axis=1)
        value = value.astype(bf16)
        for u in range(3):
            for b in range(bricks):
                stacked[
                    (u * 9 + n) * width : (u * 9 + n + 1) * width, b * wide : (b + 1) * wide
                ] = value[:, b * cube + u * LANES : b * cube + u * LANES + wide]

    def to_owner(b, e):
        peer = lax.rem(mine + e, parts)
        return pltpu.make_async_remote_copy(
            src_ref=comp.at[pl.ds(pl.multiple_of(peer * width, width), width), pl.ds(b * VOX, VOX)],
            dst_ref=sum_in.at[e, :, pl.ds(b * VOX, VOX)],
            send_sem=sum_s.at[b, e], recv_sem=sum_r.at[b, e],
            device_id=(me, peer), device_id_type=MESH,
        )

    own_rows = pl.ds(pl.multiple_of(mine * width, width), width)

    def to_all(b, e):
        peer = lax.rem(mine + e, parts)
        place_at = gates.at[own_rows, pl.ds(b * VOX, VOX)]
        return pltpu.make_async_remote_copy(
            src_ref=place_at, dst_ref=place_at,
            send_sem=gate_s.at[b, e], recv_sem=gate_r.at[b, e],
            device_id=(me, peer), device_id_type=MESH,
        )

    for b in range(bricks):
        for t in range(TILES):
            i = b * TILES + t
            part = nn_dot(w_turned[...], stacked[:, 2 * i * LANES : 2 * (i + 1) * LANES])
            comp[:, i * LANES : (i + 1) * LANES] = nt_dot(
                part.astype(bf16), expand[...]
            ).astype(bf16)
        for e in range(1, parts):
            to_owner(b, e).start()

    for b in range(bricks):
        span = slice(b * VOX, (b + 1) * VOX)
        pre = comp[own_rows, span].astype(f32)
        for e in range(1, parts):
            to_owner(b, e).wait_recv()
            pre = pre + sum_in[e, :, span].astype(f32)
        pre = pre * masks[b]
        gate = jax.nn.sigmoid(pre)
        act[:, span] = (pre * gate).astype(bf16)
        gates[own_rows, span] = (
            cot[:, span].astype(f32) * masks[b] * gate * (1.0 + pre * (1.0 - gate))
        ).astype(bf16)
        for e in range(1, parts):
            to_all(b, e).start()

    for b in range(bricks):
        for e in range(1, parts):
            to_all(b, e).wait_recv()
        for t in range(TILES):
            i = b * TILES + t
            value = nn_dot(gates[:, i * LANES : (i + 1) * LANES], expand[...]).astype(bf16)
            for u in range(3):
                at = b * cube + (u + 2 * t) * LANES
                window[u * total : (u + 1) * total, at : at + 2 * LANES] = value

    reach = owners * chunk
    for start in range(0, reach, reach // 2):
        value = None
        for b in range(bricks):
            term = nt_dot(
                stacked[start : start + reach // 2, b * wide : (b + 1) * wide],
                window[total : 2 * total, b * cube + LANES : b * cube + LANES + wide],
            )
            value = term if value is None else value + term
        gw_own[start : start + reach // 2, :] = value
        gw_send[start : start + reach // 2, :] = value.astype(bf16)

    def chunk_rows(index):
        return pl.ds(pl.multiple_of(index * chunk, 16), chunk)

    def reduce_copy(d):
        peer = lax.rem(me + d, groups)
        kept = jnp.minimum(peer, owners - 1)
        return peer, pltpu.make_async_remote_copy(
            src_ref=gw_send.at[chunk_rows(kept)], dst_ref=gw_in.at[d],
            send_sem=red_s.at[d], recv_sem=red_r.at[d],
            device_id=(peer, mine), device_id_type=MESH,
        )

    kept_me = jnp.minimum(me, owners - 1)

    def share_copy(d):
        peer = lax.rem(me + d, groups)
        span = gw_all.at[chunk_rows(kept_me)]
        return pltpu.make_async_remote_copy(
            src_ref=span, dst_ref=span, send_sem=all_s.at[d], recv_sem=all_r.at[d],
            device_id=(peer, mine), device_id_type=MESH,
        )

    def guarded(flag, action):
        if owners == groups:
            action()
        else:
            pl.when(flag)(action)

    for d in range(1, groups):
        peer, copy = reduce_copy(d)
        guarded(peer < owners, copy.start)

    for i in range(length // (2 * LANES)):
        span = slice(2 * i * LANES, 2 * (i + 1) * LANES)
        prod[:, span] = nn_dot(w_wide[...], window[:, span])
    spread = prod[0:width, :]
    for n in range(1, 9):
        spread = spread + pltpu.roll(prod[n * width : (n + 1) * width, :], shifts[n], axis=1)
    padded[...] = spread

    pieces = []
    blank = jnp.zeros((width, LANES), f32)
    for b in range(bricks):
        for t in range(TILES):
            at = b * cube + (2 * t + 1) * LANES
            pieces.append(padded[:, at : at + 2 * LANES])
    for b in range(bricks):
        pieces.append(jnp.concatenate([blank, padded[:, b * cube : b * cube + LANES]], axis=1))
    for b in range(bricks):
        at = (b + 1) * cube - LANES
        pieces.append(jnp.concatenate([padded[:, at : at + LANES], blank], axis=1))
    rims = jnp.concatenate(pieces, axis=0).astype(bf16)

    whole = TILES * width
    own = [jnp.zeros((whole, LANES), f32) for _ in range(bricks)]
    own_end = {(b, x): blank for b in range(bricks) for x in (-1, 1)}
    slots = [jnp.zeros((whole if a == 0 else width, LANES), f32) for a, _ in tile_moves]

    def picked(index, wanted, value):
        return jnp.where(jnp.full(value.shape, index, jnp.int32) == wanted, value, 0.0)

    for n, (y, z) in enumerate(plane_offsets):
        folded = nt_dot(rims, place[n])
        for x in (-1, 0, 1):
            slot = None if (x, y) == (0, 0) else tile_moves.index((x, y))
            for b in range(bricks):
                if x == 0:
                    piece = folded[b * whole : (b + 1) * whole]
                else:
                    at = ends + (b if x == -1 else bricks + b) * width
                    piece = folded[at : at + width]
                if (x, y, z) == (0, 0, 0):
                    own[b] = own[b] + piece
                    continue
                index = near[b, neighbour_slot(x, y, z)]
                for c in range(bricks):
                    term = picked(index, c, piece)
                    if x == 0:
                        own[c] = own[c] + term
                    else:
                        own_end[c, x] = own_end[c, x] + term
                if slot is not None:
                    slots[slot] = slots[slot] + picked(index, bricks + slot, piece)
    for k, (a, _) in enumerate(tile_moves):
        if a == 0:
            backbox[k] = slots[k].astype(bf16).reshape(TILES, width, LANES)
        else:
            backbox[k, tile_of(a)] = slots[k].astype(bf16)
        start_if(ahead[k], back[k])

    def add_up():
        value = gw_own[chunk_rows(kept_me), :]
        for d in range(1, groups):
            reduce_copy(d)[1].wait_recv()
            value = value + gw_in[d].astype(f32)
        gw_all[chunk_rows(kept_me), :] = (value * scale).astype(bf16)
        for d in range(1, groups):
            share_copy(d).start()

    guarded(me < owners, add_up)

    for k in range(8):
        arrived_if(behind[k], back[k])
    for b in range(bricks):
        for t in range(TILES):
            value = own[b][t * width : (t + 1) * width]
            for x in (-1, 1):
                if t == tile_of(x):
                    value = value + own_end[b, x]
            for k, (a, _) in enumerate(tile_moves):
                if a == 0 or t == tile_of(a):
                    value = value + picked(sends[0, k, 0], b, back_in[k, t].astype(f32))
            at = b * VOX + t * LANES
            grad_feat[:, at : at + LANES] = (
                value * masks[b][:, t * LANES : (t + 1) * LANES]
            ).astype(bf16)

    for d in range(1, groups):
        source = lax.rem(me + groups - d, groups)
        guarded(source < owners, share_copy(d).wait_recv)
    grad_w[...] = gw_all[0:rows_w, :].astype(f32)

    for k in range(8):
        sent_if(behind[k], forth[k])
        sent_if(ahead[k], back[k])
    for b in range(bricks):
        for e in range(1, parts):
            to_owner(b, e).wait_send()
            to_all(b, e).wait_send()
    for d in range(1, groups):
        peer, copy = reduce_copy(d)
        guarded(peer < owners, copy.wait_send)
        guarded(me < owners, share_copy(d).wait_send)


def on_device(features, mask_packed, neighbours, send_list, weights, cotangent):
    groups, parts = lax.axis_size("space"), lax.axis_size("chan")
    width, bricks = features.shape[0], features.shape[1]
    total = weights.shape[2]
    rows_w = 27 * width
    chunk, owners = plan_chunks(rows_w, groups)
    rows_k = -(-max(rows_w, owners * chunk) // LANES) * LANES
    wide, cube = BRICK * LANES, PLANES * LANES
    scale = 1.0 / math.sqrt(bricks * groups * VOX)
    f32, bf16 = jnp.float32, jnp.bfloat16
    vmem = pl.BlockSpec(memory_space=pltpu.VMEM)
    smem = pl.BlockSpec(memory_space=pltpu.SMEM)
    dma = pltpu.SemaphoreType.DMA
    act, grad_feat, grad_w = pl.pallas_call(
        functools.partial(kernel, groups, parts, width, bricks, scale),
        out_shape=(
            jax.ShapeDtypeStruct((width, bricks * VOX), bf16),
            jax.ShapeDtypeStruct((width, bricks * VOX), bf16),
            jax.ShapeDtypeStruct((rows_w, total), f32),
        ),
        in_specs=[smem, smem, smem, vmem, vmem, vmem],
        out_specs=(vmem, vmem, vmem),
        scratch_shapes=[
            pltpu.VMEM((bricks + 9, TILES, width, LANES), bf16),
            pltpu.VMEM((8, TILES, width, LANES), bf16),
            pltpu.VMEM((9, LANES, 2 * LANES), bf16),
            pltpu.VMEM((LANES, 2 * LANES), bf16),
            pltpu.VMEM((total, rows_k), bf16),
            pltpu.VMEM((9 * width, 3 * total), bf16),
            pltpu.VMEM((width, bricks * cube), f32),
            pltpu.VMEM((rows_k, bricks * wide), bf16),
            pltpu.VMEM((total, bricks * VOX), bf16),
            pltpu.VMEM((parts, width, bricks * VOX), bf16),
            pltpu.VMEM((total, bricks * VOX), bf16),
            pltpu.VMEM((3 * total, bricks * cube), bf16),
            pltpu.VMEM((9 * width, bricks * cube), f32),
            pltpu.VMEM((8, TILES, width, LANES), bf16),
            pltpu.VMEM((8, TILES, width, LANES), bf16),
            pltpu.VMEM((owners * chunk, total), f32),
            pltpu.VMEM((owners * chunk, total), bf16),
            pltpu.VMEM((groups, chunk, total), bf16),
            pltpu.VMEM((owners * chunk, total), bf16),
            dma((8,)), dma((8,)), dma((8,)), dma((8,)),
            dma((bricks, parts)), dma((bricks, parts)), dma((bricks, parts)), dma((bricks, parts)),
            dma((groups,)), dma((groups,)), dma((groups,)), dma((groups,)),
        ],
        compiler_params=pltpu.CompilerParams(
            collective_id=0, has_side_effects=True, vmem_limit_bytes=40 * 2**20
        ),
    )(
        mask_packed, neighbours, send_list,
        features.reshape(width, bricks * VOX), weights.reshape(rows_w, total),
        cotangent.reshape(width, bricks * VOX),
    )
    shape = (width, bricks, VOX)
    return act.reshape(shape), grad_feat.reshape(shape), grad_w.reshape(27, width, total)


def solution(mesh):
    return jax.shard_map(
        on_device,
        mesh=mesh,
        in_specs=(
            P("chan", "space", None),
            P("space", None),
            P("space", None),
            P("space", None, None),
            P(None, "chan", None),
            P("chan", "space", None),
        ),
        out_specs=(P("chan", "space", None), P("chan", "space", None), P(None, "chan", None)),
        check_vma=False,
    )
```

time: 720 us -> 41.2 us (0.06); the launches traced: 712 us -> 41 us
  local copies, waits for them, and re-layouts: 328 us -> 5.22 us
  other arithmetic: 229 us -> 0 us
  waiting for transfers between devices: 78.5 us -> 0 us
  Pallas kernels: 0 us -> 35.1 us
  starting transfers between devices: 34.6 us -> 0 us
  between operations: 31.2 us -> 0.69 us
    scatter-add x208 -> x0, local copies, waits for them, and re-layouts: 267 us -> none
    scatter-add x105 -> x0, other arithmetic: 213 us -> none
    psum x1 -> x0, waiting for transfers between devices: 54.6 us -> none  [on_device(): lax.psum(grad_weight, 'space') * grad_scale]
    pallas_call x0 -> x1, Pallas kernels: none -> 35.1 us  [on_device(): pl.pallas_call(functools.partial(kernel, groups, parts, width, bricks, sc...]
    ppermute x16 -> x0, starting transfers between devices: 34.5 us -> none  [passed_along(): return lax.ppermute(shard, axis, pairs)]
    ppermute x16 -> x0, waiting for transfers between devices: 14.3 us -> none  [passed_along(): return lax.ppermute(shard, axis, pairs)]
    gather x26 -> x0, local copies, waits for them, and re-layouts: 14.3 us -> none  [assemble(): jnp.take(source_table, indices[:, neighbour_slot(along_x, along_y, along_...]
    slice x44 -> x0, local copies, waits for them, and re-layouts: 12.8 us -> none  [the longest x7 3.9 us: scatter_block(): padded_cube[:, :, cycle_slice(along_x, extent), cycle_slice(along_y, exte...]
  transfers between devices with their start and end apart: 18 -> 0, of which waited for: 7 -> 0; matrix products, arithmetic and copies ran while one was open for 5% -> 0% of each run, Pallas kernels for 0% -> 0%
where the time goes in v1:
time: 41.2 us; the launch traced here: 41 us
  Pallas kernels  35.1 us (85%)
  local copies, waits for them, and re-layouts  5.22 us (13%)
  between operations  0.69 us (2%)
    pallas_call x1, Pallas kernels, on_device(): pl.pallas_call(functools.partial(kernel, groups, parts, width, bricks, sc...  35.1 us
    unnamed x10, local copies, waits for them, and re-layouts  3.9 us

profile of v1, /device:TPU:0, one launch (start us, length us, event | category | flops | bytes accessed | tf_op | source)
XLA Modules:
  0.0 41.0 jit_solution(1557502735859758247)
XLA Ops:
  0.6 0.0 copy-start
  0.6 0.8 %copy.9.sends = s32[1,8,1]{2,1,0:T(8,128)S(1)} copy(s32[1,8,1]{1,2,0:T(1,128)} %param.9) | data formatting | bytes 64 | tf_op args[3]
  1.4 0.8 %copy.10 = bf16[4,8,2,512]{3,1,2,0:T(8,128)(2,1)S(1)} copy(bf16[4,8,2,512]{3,2,1,0:T(2,128)(2,1)} %bitcast.10) | data formatting | bytes 131072
  2.3 0.0 copy-start.2
  2.3 0.9 %copy.11 = bf16[4,8,2,512]{3,1,2,0:T(8,128)(2,1)S(1)} copy(bf16[4,8,2,512]{3,2,1,0:T(2,128)(2,1)} %bitcast.11) | data formatting | bytes 131072
  3.1 0.0 copy-start.1
  3.1 0.0 copy-done
  3.2 0.0 copy-done.2
  3.2 0.7 %copy-done.1 = s32[2,16]{1,0:T(2,128)S(1)} copy-done((s32[2,16]{1,0:T(2,128)S(1)}, s32[2,16]{1,0:T(2,128)}, u32[]{:S(2)}) %copy-start.1) | copy-done | bytes 152
  3.8 35.1 %shard_map.85 = (bf16[32,1024]{1,0:T(8,128)(2,1)S(1)}, bf16[32,1024]{1,0:T(8,128)(2,1)S(1)}, f32[864,128]{1,0:T(8,128)S(1)}) custom-call(s32[2,16]{1,0:T(2,128)S(1)} %copy-done.1, s32[2,26]{1,0:T(2,128)S(1)} %copy-done.2, s32[1,8,1]{2,1,0:T(8,128)S(1)} %copy.9.sends, bf16[32,1024]{1,0:T(8,128)(2,1)S(1)} %bitcast.7, bf16[864,128]{1,0:T(8,128)(2,1)S(1)} %bitcast.9, ...), custom_call_target="tpu_custom_call" | custom-call | tf_op jit(solution)/shard_map/pallas_call | solution.py:433
  38.9 0.7 %reshape.27 = bf16[32,2,512]{2,1,0:T(2,128)(2,1)} reshape(bf16[32,1024]{1,0:T(8,128)(2,1)S(1)} %get-tuple-element.6) | data formatting | bytes 131072 | tf_op jit(solution)/shard_map/reshape | solution.py:475
  39.6 0.7 %reshape.28 = bf16[32,2,512]{2,1,0:T(2,128)(2,1)} reshape(bf16[32,1024]{1,0:T(8,128)(2,1)S(1)} %get-tuple-element.7) | data formatting | bytes 131072 | tf_op jit(solution)/shard_map/reshape | solution.py:475
  40.3 0.8 %copy.13 = f32[27,32,128]{2,1,0:T(8,128)} copy(f32[27,32,128]{2,1,0:T(8,128)S(1)} %bitcast.6) | data formatting | bytes 884736
Async XLA Ops:
  0.6 2.5 %copy-start = (bf16[27,32,128]{2,1,0:T(8,128)(2,1)S(1)}, bf16[27,32,128]{2,1,0:T(8,128)(2,1)}, u32[]{:S(2)}) copy-start(bf16[27,32,128]{2,1,0:T(8,128)(2,1)} %param.10) | copy-start | bytes 663556
  2.3 0.9 %copy-start.2 = (s32[2,26]{1,0:T(2,128)S(1)}, s32[2,26]{1,0:T(2,128)}, u32[]{:S(2)}) copy-start(s32[2,26]{1,0:T(2,128)} %near.1) | copy-start | bytes 628
  3.1 0.7 %copy-start.1 = (s32[2,16]{1,0:T(2,128)S(1)}, s32[2,16]{1,0:T(2,128)}, u32[]{:S(2)}) copy-start(s32[2,16]{1,0:T(2,128)} %packed.1) | copy-start | bytes 388

commit v2 on v1

--- a/solution.py
+++ b/solution.py
@@ -80,14 +80,14 @@
         masks.append((lax.shift_right_logical(word, lane & 31) & 1).astype(f32))
 
     masked = [
-        feat[:, b * VOX : (b + 1) * VOX].astype(f32) * masks[b] for b in range(bricks)
+        feat[:, b, :].astype(f32) * masks[b] for b in range(bricks)
     ]
     for b in range(bricks):
         for t in range(TILES):
             table[b, t] = masked[b][:, t * LANES : (t + 1) * LANES].astype(bf16)
     table[bricks + 8] = jnp.zeros((TILES, width, LANES), bf16)
     for k, (a, _) in enumerate(tile_moves):
-        chosen = jnp.full((width, LANES), sends[0, k, 0], jnp.int32)
+        chosen = jnp.full((width, LANES), sends[0, k], jnp.int32)
         for t in range(TILES) if a == 0 else (tile_of(a),):
             value = jnp.zeros((width, LANES), f32)
             for b in range(bricks):
@@ -150,7 +150,7 @@
             hit = hit & side_y[y]
         if z != 0:
             hit = hit & side_z[z]
-        place[n] = jnp.where(hit, 1.0, 0.0).astype(bf16)
+        place[n * LANES : (n + 1) * LANES, :] = jnp.where(hit, 1.0, 0.0).astype(bf16)
     expand[...] = jnp.where(col == goal - (PLANES + 1), 1.0, 0.0).astype(bf16)
 
     rows_k = w_turned.shape[1]
@@ -179,7 +179,7 @@
     for k in range(8):
         arrived_if(ahead[k], forth[k])
 
-    built = jnp.zeros((bricks * (TILES + 2) * width, 2 * LANES), f32)
+    columns = []
     for n, (y, z) in enumerate(plane_offsets):
         pieces = []
         for b in range(bricks):
@@ -188,7 +188,8 @@
         for x in (-1, 1):
             for b in range(bricks):
                 pieces.append(table[near[b, neighbour_slot(x, y, z)], tile_of(x)])
-        built = built + nn_dot(jnp.concatenate(pieces, axis=0), place[n])
+        columns.append(jnp.concatenate(pieces, axis=0))
+    built = nn_dot(jnp.concatenate(columns, axis=1), place[...])
     ends = bricks * TILES * width
     for b in range(bricks):
         base = b * cube
@@ -255,7 +256,7 @@
         gate = jax.nn.sigmoid(pre)
         act[:, span] = (pre * gate).astype(bf16)
         gates[own_rows, span] = (
-            cot[:, span].astype(f32) * masks[b] * gate * (1.0 + pre * (1.0 - gate))
+            cot[:, b, :].astype(f32) * masks[b] * gate * (1.0 + pre * (1.0 - gate))
         ).astype(bf16)
         for e in range(1, parts):
             to_all(b, e).start()
@@ -269,18 +270,6 @@
             for u in range(3):
                 at = b * cube + (u + 2 * t) * LANES
                 window[u * total : (u + 1) * total, at : at + 2 * LANES] = value
-
-    reach = owners * chunk
-    for start in range(0, reach, reach // 2):
-        value = None
-        for b in range(bricks):
-            term = nt_dot(
-                stacked[start : start + reach // 2, b * wide : (b + 1) * wide],
-                window[total : 2 * total, b * cube + LANES : b * cube + LANES + wide],
-            )
-            value = term if value is None else value + term
-        gw_own[start : start + reach // 2, :] = value
-        gw_send[start : start + reach // 2, :] = value.astype(bf16)
 
     def chunk_rows(index):
         return pl.ds(pl.multiple_of(index * chunk, 16), chunk)
@@ -310,9 +299,26 @@
         else:
             pl.when(flag)(action)
 
-    for d in range(1, groups):
-        peer, copy = reduce_copy(d)
-        guarded(peer < owners, copy.start)
+    pack = 2 if owners % 2 == 0 else 1
+    packs = owners // pack
+    for i in range(packs):
+        first = lax.rem(me // pack + i + 1, packs) * pack
+        span = pl.ds(pl.multiple_of(first * chunk, 16), pack * chunk)
+        value = None
+        for b in range(bricks):
+            term = nt_dot(
+                stacked[span, b * wide : (b + 1) * wide],
+                window[total : 2 * total, b * cube + LANES : b * cube + LANES + wide],
+            )
+            value = term if value is None else value + term
+        gw_own[span, :] = value
+        gw_send[span, :] = value.astype(bf16)
+        for c in range(pack):
+            copy = reduce_copy(lax.rem(first + c - me + groups, groups))[1]
+            if groups == owners and i < packs - 1:
+                copy.start()
+            else:
+                pl.when(first + c != me)(copy.start)
 
     for i in range(length // (2 * LANES)):
         span = slice(2 * i * LANES, 2 * (i + 1) * LANES)
@@ -344,7 +350,7 @@
         return jnp.where(jnp.full(value.shape, index, jnp.int32) == wanted, value, 0.0)
 
     for n, (y, z) in enumerate(plane_offsets):
-        folded = nt_dot(rims, place[n])
+        folded = nt_dot(rims, place[n * LANES : (n + 1) * LANES, :])
         for x in (-1, 0, 1):
             slot = None if (x, y) == (0, 0) else tile_moves.index((x, y))
             for b in range(bricks):
@@ -393,7 +399,7 @@
                     value = value + own_end[b, x]
             for k, (a, _) in enumerate(tile_moves):
                 if a == 0 or t == tile_of(a):
-                    value = value + picked(sends[0, k, 0], b, back_in[k, t].astype(f32))
+                    value = value + picked(sends[0, k], b, back_in[k, t].astype(f32))
             at = b * VOX + t * LANES
             grad_feat[:, at : at + LANES] = (
                 value * masks[b][:, t * LANES : (t + 1) * LANES]
@@ -442,7 +448,7 @@
         scratch_shapes=[
             pltpu.VMEM((bricks + 9, TILES, width, LANES), bf16),
             pltpu.VMEM((8, TILES, width, LANES), bf16),
-            pltpu.VMEM((9, LANES, 2 * LANES), bf16),
+            pltpu.VMEM((9 * LANES, 2 * LANES), bf16),
             pltpu.VMEM((LANES, 2 * LANES), bf16),
             pltpu.VMEM((total, rows_k), bf16),
             pltpu.VMEM((9 * width, 3 * total), bf16),
@@ -467,9 +473,8 @@
             collective_id=0, has_side_effects=True, vmem_limit_bytes=40 * 2**20
         ),
     )(
-        mask_packed, neighbours, send_list,
-        features.reshape(width, bricks * VOX), weights.reshape(rows_w, total),
-        cotangent.reshape(width, bricks * VOX),
+        mask_packed, neighbours, send_list.reshape(1, 8),
+        features, weights.reshape(rows_w, total), cotangent,
     )
     shape = (width, bricks, VOX)
     return act.reshape(shape), grad_feat.reshape(shape), grad_w.reshape(27, width, total)

time: 41.2 us -> 40.2 us (0.976)
  Pallas kernels: 35.1 us -> 33.9 us
    pallas_call x1, Pallas kernels: 35.1 us -> 33.9 us  [on_device(): pl.pallas_call(functools.partial(kernel, groups, parts, width, bricks, sc...]
    unnamed x10 -> x13, local copies, waits for them, and re-layouts: 3.9 us -> 4.05 us
where the time goes in v2:
time: 40.2 us; the launch traced here: 39.9 us
  Pallas kernels  33.9 us (84%)
  local copies, waits for them, and re-layouts  5.37 us (13%)
  between operations  0.67 us (2%)
    pallas_call x1, Pallas kernels, on_device(): pl.pallas_call(functools.partial(kernel, groups, parts, width, bricks, sc...  33.9 us
    unnamed x13, local copies, waits for them, and re-layouts  4.05 us

profile of v2, /device:TPU:0, one launch (start us, length us, event | category | flops | bytes accessed | tf_op | source)
XLA Modules:
  0.0 39.9 jit_solution(7352820299665115262)
XLA Ops:
  0.6 0.0 copy-start.4
  0.6 0.0 copy-start.3
  0.7 0.0 copy-start.5
  0.7 0.7 %copy-done.4 = s32[2,26]{1,0:T(2,128)S(1)} copy-done((s32[2,26]{1,0:T(2,128)S(1)}, s32[2,26]{1,0:T(2,128)}, u32[]{:S(2)}) %copy-start.4) | copy-done | bytes 232
  1.3 0.0 copy-done.3
  1.3 0.0 copy-done.5
  1.3 0.0 copy-start
  1.3 0.9 %copy-done = bf16[27,32,128]{2,1,0:T(8,128)(2,1)S(1)} copy-done((bf16[27,32,128]{2,1,0:T(8,128)(2,1)S(1)}, bf16[27,32,128]{2,1,0:T(8,128)(2,1)}, u32[]{:S(2)}) %copy-start) | copy-done | bytes 221208
  2.3 0.0 copy-start.1
  2.3 0.8 %copy-done.1 = bf16[32,2,512]{2,1,0:T(2,128)(2,1)S(1)} copy-done((bf16[32,2,512]{2,1,0:T(2,128)(2,1)S(1)}, bf16[32,2,512]{2,1,0:T(2,128)(2,1)}, u32[]{:S(2)}) %copy-start.1) | copy-done | bytes 65560
  3.1 0.0 copy-start.2
  3.1 0.8 %copy-done.2 = bf16[32,2,512]{2,1,0:T(2,128)(2,1)S(1)} copy-done((bf16[32,2,512]{2,1,0:T(2,128)(2,1)S(1)}, bf16[32,2,512]{2,1,0:T(2,128)(2,1)}, u32[]{:S(2)}) %copy-start.2) | copy-done | bytes 65560
  3.9 33.9 %shard_map.85 = (bf16[32,1024]{1,0:T(8,128)(2,1)S(1)}, bf16[32,1024]{1,0:T(8,128)(2,1)S(1)}, f32[864,128]{1,0:T(8,128)S(1)}) custom-call(s32[2,16]{1,0:T(2,128)S(1)} %copy-done.3, s32[2,26]{1,0:T(2,128)S(1)} %copy-done.4, s32[1,8]{1,0:T(1,128)S(1)} %bitcast.5, bf16[32,2,512]{2,1,0:T(2,128)(2,1)S(1)} %copy-done.1, bf16[864,128]{1,0:T(8,128)(2,1)S(1)} %bitcast.4, ...), custom_call_target="tpu_custom_call" | custom-call | tf_op jit(solution)/shard_map/pallas_call | solution.py:439
  37.8 0.7 %reshape.23 = bf16[32,2,512]{2,1,0:T(2,128)(2,1)} reshape(bf16[32,1024]{1,0:T(8,128)(2,1)S(1)} %get-tuple-element.6) | data formatting | bytes 131072 | tf_op jit(solution)/shard_map/reshape | solution.py:480
  38.5 0.7 %reshape.24 = bf16[32,2,512]{2,1,0:T(2,128)(2,1)} reshape(bf16[32,1024]{1,0:T(8,128)(2,1)S(1)} %get-tuple-element.7) | data formatting | bytes 131072 | tf_op jit(solution)/shard_map/reshape | solution.py:480
  39.1 0.8 %copy.10 = f32[27,32,128]{2,1,0:T(8,128)} copy(f32[27,32,128]{2,1,0:T(8,128)S(1)} %bitcast.3) | data formatting | bytes 884736
Async XLA Ops:
  0.6 0.7 %copy-start.4 = (s32[2,26]{1,0:T(2,128)S(1)}, s32[2,26]{1,0:T(2,128)}, u32[]{:S(2)}) copy-start(s32[2,26]{1,0:T(2,128)} %near.1) | copy-start | bytes 628
  0.6 0.7 %copy-start.3 = (s32[2,16]{1,0:T(2,128)S(1)}, s32[2,16]{1,0:T(2,128)}, u32[]{:S(2)}) copy-start(s32[2,16]{1,0:T(2,128)} %packed.1) | copy-start | bytes 388
  0.7 0.7 %copy-start.5 = (s32[1,8,1]{1,2,0:T(1,128)S(1)}, s32[1,8,1]{1,2,0:T(1,128)}, u32[]{:S(2)}) copy-start(s32[1,8,1]{1,2,0:T(1,128)} %param.9) | copy-start | bytes 100
  1.3 0.9 %copy-start = (bf16[27,32,128]{2,1,0:T(8,128)(2,1)S(1)}, bf16[27,32,128]{2,1,0:T(8,128)(2,1)}, u32[]{:S(2)}) copy-start(bf16[27,32,128]{2,1,0:T(8,128)(2,1)} %param.10) | copy-start | bytes 663556
  2.3 0.8 %copy-start.1 = (bf16[32,2,512]{2,1,0:T(2,128)(2,1)S(1)}, bf16[32,2,512]{2,1,0:T(2,128)(2,1)}, u32[]{:S(2)}) copy-start(bf16[32,2,512]{2,1,0:T(2,128)(2,1)} %feat.1) | copy-start | bytes 196612
  3.1 0.8 %copy-start.2 = (bf16[32,2,512]{2,1,0:T(2,128)(2,1)S(1)}, bf16[32,2,512]{2,1,0:T(2,128)(2,1)}, u32[]{:S(2)}) copy-start(bf16[32,2,512]{2,1,0:T(2,128)(2,1)} %cot.1) | copy-start | bytes 196612

commit v3 on v2

--- a/solution.py
+++ b/solution.py
@@ -47,11 +47,12 @@
 
 def kernel(
     groups, parts, width, bricks, scale,
-    packed, near, sends, feat, w, cot,
-    act, grad_feat, grad_w,
-    table, outbox, place, expand, w_turned, w_wide, padded, stacked, comp, sum_in, gates,
+    packed_in, near_in, sends_in, feat_in, w_in, cot_in,
+    act_out, grad_feat_out, grad_w_out,
+    packed, near, sends, feat, w, cot, act, grad_feat, grad_w, in_s, out_s,
+    table, outbox, place, expand, w_turned, w_wide, padded, stacked, comp, mate_in, halves, cross_in, cots, gates,
     window, prod, backbox, back_in, gw_own, gw_send, gw_in, gw_all,
-    halo_s, halo_r, back_s, back_r, sum_s, sum_r, gate_s, gate_r, red_s, red_r, all_s, all_r,
+    halo_s, halo_r, back_s, back_r, mate_s, mate_r, cross_s, cross_r, gate_s, gate_r, cot_s, cot_r, red_s, red_r, all_s, all_r,
 ):
     me, mine = lax.axis_index("space"), lax.axis_index("chan")
     total = parts * width
@@ -61,15 +62,29 @@
     cube = PLANES * LANES
     f32, bf16 = jnp.float32, jnp.bfloat16
 
+    fetches = [
+        pltpu.make_async_copy(source, target, in_s.at[i])
+        for i, (source, target) in enumerate(
+            (
+                (packed_in, packed), (feat_in, feat), (sends_in, sends), (near_in, near),
+                (cot_in, cot), (w_in, w),
+            )
+        )
+    ]
+    for fetch in fetches:
+        fetch.start()
+    level, low = mine // 2, lax.rem(mine, 2)
+    mate, across = mine + 1 - 2 * low, lax.rem(mine + 2, 4)
+
     barrier = pltpu.get_barrier_semaphore()
     for d in range(1, groups):
         pl.semaphore_signal(
             barrier, inc=1, device_id=(lax.rem(me + d, groups), mine), device_id_type=MESH
         )
-    for e in range(1, parts):
-        pl.semaphore_signal(
-            barrier, inc=1, device_id=(me, lax.rem(mine + e, parts)), device_id_type=MESH
-        )
+    for peer in (mate, across):
+        pl.semaphore_signal(barrier, inc=1, device_id=(me, peer), device_id_type=MESH)
+    for fetch in fetches[:3]:
+        fetch.wait()
 
     lane = lax.broadcasted_iota(jnp.int32, (1, VOX), 1)
     masks = []
@@ -94,7 +109,7 @@
                 value = jnp.where(chosen == b, masked[b][:, t * LANES : (t + 1) * LANES], value)
             outbox[k, t] = value.astype(bf16)
 
-    pl.semaphore_wait(barrier, groups - 1 + parts - 1)
+    pl.semaphore_wait(barrier, groups - 1 + 2)
 
     tile_a, tile_b = me // 4, lax.rem(me, 4)
 
@@ -137,6 +152,16 @@
 
     for k in range(8):
         start_if(behind[k], forth[k])
+
+    for fetch in fetches[3:]:
+        fetch.wait()
+    for b in range(bricks):
+        cots[level, :, b * VOX : (b + 1) * VOX] = cot[:, b, :]
+    cot_copy = pltpu.make_async_remote_copy(
+        src_ref=cots.at[level], dst_ref=cots.at[level], send_sem=cot_s.at[0],
+        recv_sem=cot_r.at[0], device_id=(me, across), device_id_type=MESH,
+    )
+    cot_copy.start()
 
     row = lax.broadcasted_iota(jnp.int32, (LANES, 2 * LANES), 0)
     col = lax.broadcasted_iota(jnp.int32, (LANES, 2 * LANES), 1)
@@ -193,10 +218,10 @@
     ends = bricks * TILES * width
     for b in range(bricks):
         base = b * cube
-        low = ends + b * width
-        high = ends + (bricks + b) * width
-        padded[:, base : base + LANES] = built[low : low + width, LANES:]
-        padded[:, base + cube - LANES : base + cube] = built[high : high + width, :LANES]
+        first = ends + b * width
+        last = ends + (bricks + b) * width
+        padded[:, base : base + LANES] = built[first : first + width, LANES:]
+        padded[:, base + cube - LANES : base + cube] = built[last : last + width, :LANES]
         for t in range(TILES):
             at = (b * TILES + t) * width
             padded[:, base + (2 * t + 1) * LANES : base + (2 * t + 3) * LANES] = built[
@@ -216,57 +241,78 @@
                     (u * 9 + n) * width : (u * 9 + n + 1) * width, b * wide : (b + 1) * wide
                 ] = value[:, b * cube + u * LANES : b * cube + u * LANES + wide]
 
-    def to_owner(b, e):
-        peer = lax.rem(mine + e, parts)
+    def chan_copy(source, target, send, recv, peer):
         return pltpu.make_async_remote_copy(
-            src_ref=comp.at[pl.ds(pl.multiple_of(peer * width, width), width), pl.ds(b * VOX, VOX)],
-            dst_ref=sum_in.at[e, :, pl.ds(b * VOX, VOX)],
-            send_sem=sum_s.at[b, e], recv_sem=sum_r.at[b, e],
+            src_ref=source, dst_ref=target, send_sem=send, recv_sem=recv,
             device_id=(me, peer), device_id_type=MESH,
         )
 
-    own_rows = pl.ds(pl.multiple_of(mine * width, width), width)
-
-    def to_all(b, e):
-        peer = lax.rem(mine + e, parts)
-        place_at = gates.at[own_rows, pl.ds(b * VOX, VOX)]
-        return pltpu.make_async_remote_copy(
-            src_ref=place_at, dst_ref=place_at,
-            send_sem=gate_s.at[b, e], recv_sem=gate_r.at[b, e],
-            device_id=(me, peer), device_id_type=MESH,
-        )
+    spans = [pl.ds(b * VOX, VOX) for b in range(bricks)]
+    to_mate = [
+        chan_copy(
+            comp.at[:, 1 - low, :, spans[b]], mate_in.at[:, :, spans[b]],
+            mate_s.at[b], mate_r.at[b], mate,
+        )
+        for b in range(bricks)
+    ]
+    to_across = [
+        chan_copy(
+            halves.at[:, :, spans[b]], cross_in.at[:, :, spans[b]],
+            cross_s.at[b], cross_r.at[b], across,
+        )
+        for b in range(bricks)
+    ]
+    to_both = [
+        chan_copy(
+            gates.at[:, low, :, spans[b]], gates.at[:, low, :, spans[b]],
+            gate_s.at[b], gate_r.at[b], mate,
+        )
+        for b in range(bricks)
+    ]
 
     for b in range(bricks):
         for t in range(TILES):
             i = b * TILES + t
             part = nn_dot(w_turned[...], stacked[:, 2 * i * LANES : 2 * (i + 1) * LANES])
-            comp[:, i * LANES : (i + 1) * LANES] = nt_dot(
-                part.astype(bf16), expand[...]
+            comp[:, :, :, i * LANES : (i + 1) * LANES] = (
+                nt_dot(part.astype(bf16), expand[...])
+                .astype(bf16)
+                .reshape(2, 2, width, LANES)
+            )
+        to_mate[b].start()
+
+    for b in range(bricks):
+        to_mate[b].wait_recv()
+        halves[:, :, spans[b]] = (
+            comp[:, low, :, spans[b]].astype(f32) + mate_in[:, :, spans[b]].astype(f32)
+        ).astype(bf16)
+        to_across[b].start()
+
+    cot_copy.wait_recv()
+    for b in range(bricks):
+        to_across[b].wait_recv()
+        for h in range(2):
+            pre = halves[h, :, spans[b]].astype(f32) + cross_in[h, :, spans[b]].astype(f32)
+            pre = pre * masks[b]
+            gate = jax.nn.sigmoid(pre)
+            gates[h, low, :, spans[b]] = (
+                cots[h, :, spans[b]].astype(f32) * masks[b] * gate * (1.0 + pre * (1.0 - gate))
             ).astype(bf16)
-        for e in range(1, parts):
-            to_owner(b, e).start()
-
-    for b in range(bricks):
-        span = slice(b * VOX, (b + 1) * VOX)
-        pre = comp[own_rows, span].astype(f32)
-        for e in range(1, parts):
-            to_owner(b, e).wait_recv()
-            pre = pre + sum_in[e, :, span].astype(f32)
-        pre = pre * masks[b]
-        gate = jax.nn.sigmoid(pre)
-        act[:, span] = (pre * gate).astype(bf16)
-        gates[own_rows, span] = (
-            cot[:, b, :].astype(f32) * masks[b] * gate * (1.0 + pre * (1.0 - gate))
-        ).astype(bf16)
-        for e in range(1, parts):
-            to_all(b, e).start()
-
-    for b in range(bricks):
-        for e in range(1, parts):
-            to_all(b, e).wait_recv()
+
+            @pl.when(level == h)
+            def _():
+                act[:, b, :] = (pre * gate).astype(bf16)
+
+        to_both[b].start()
+    act_copy = pltpu.make_async_copy(act, act_out, out_s.at[0])
+    act_copy.start()
+
+    for b in range(bricks):
+        to_both[b].wait_recv()
         for t in range(TILES):
             i = b * TILES + t
-            value = nn_dot(gates[:, i * LANES : (i + 1) * LANES], expand[...]).astype(bf16)
+            value = gates[:, :, :, i * LANES : (i + 1) * LANES].reshape(total, LANES)
+            value = nn_dot(value, expand[...]).astype(bf16)
             for u in range(3):
                 at = b * cube + (u + 2 * t) * LANES
                 window[u * total : (u + 1) * total, at : at + 2 * LANES] = value
@@ -392,6 +438,7 @@
     for k in range(8):
         arrived_if(behind[k], back[k])
     for b in range(bricks):
+        rows = []
         for t in range(TILES):
             value = own[b][t * width : (t + 1) * width]
             for x in (-1, 1):
@@ -400,27 +447,44 @@
             for k, (a, _) in enumerate(tile_moves):
                 if a == 0 or t == tile_of(a):
                     value = value + picked(sends[0, k], b, back_in[k, t].astype(f32))
-            at = b * VOX + t * LANES
-            grad_feat[:, at : at + LANES] = (
-                value * masks[b][:, t * LANES : (t + 1) * LANES]
-            ).astype(bf16)
+            rows.append((value * masks[b][:, t * LANES : (t + 1) * LANES]).astype(bf16))
+        grad_feat[:, b, :] = jnp.concatenate(rows, axis=1)
+    feat_copy = pltpu.make_async_copy(grad_feat, grad_feat_out, out_s.at[1])
+    feat_copy.start()
 
     for d in range(1, groups):
         source = lax.rem(me + groups - d, groups)
         guarded(source < owners, share_copy(d).wait_recv)
     grad_w[...] = gw_all[0:rows_w, :].astype(f32)
+    w_copy = pltpu.make_async_copy(grad_w, grad_w_out, out_s.at[2])
+    w_copy.start()
 
     for k in range(8):
         sent_if(behind[k], forth[k])
         sent_if(ahead[k], back[k])
     for b in range(bricks):
-        for e in range(1, parts):
-            to_owner(b, e).wait_send()
-            to_all(b, e).wait_send()
+        to_mate[b].wait_send()
+        to_across[b].wait_send()
+        to_both[b].wait_send()
+    cot_copy.wait_send()
     for d in range(1, groups):
         peer, copy = reduce_copy(d)
         guarded(peer < owners, copy.wait_send)
         guarded(me < owners, share_copy(d).wait_send)
+    act_copy.wait()
+    feat_copy.wait()
+    w_copy.wait()
+
+
+def hand_over(*refs):
+    sources, targets, sem = refs[:3], refs[3:6], refs[6]
+    copies = [
+        pltpu.make_async_copy(sources[i], targets[i], sem.at[i]) for i in range(3)
+    ]
+    for copy in copies:
+        copy.start()
+    for copy in copies:
+        copy.wait()
 
 
 def on_device(features, mask_packed, neighbours, send_list, weights, cotangent):
@@ -433,19 +497,29 @@
     wide, cube = BRICK * LANES, PLANES * LANES
     scale = 1.0 / math.sqrt(bricks * groups * VOX)
     f32, bf16 = jnp.float32, jnp.bfloat16
-    vmem = pl.BlockSpec(memory_space=pltpu.VMEM)
-    smem = pl.BlockSpec(memory_space=pltpu.SMEM)
     dma = pltpu.SemaphoreType.DMA
-    act, grad_feat, grad_w = pl.pallas_call(
+    outputs = (
+        jax.ShapeDtypeStruct((width, bricks, VOX), bf16),
+        jax.ShapeDtypeStruct((width, bricks, VOX), bf16),
+        jax.ShapeDtypeStruct((rows_w, total), f32),
+    )
+    anywhere = pl.BlockSpec(memory_space=pl.ANY)
+    results = pl.pallas_call(
         functools.partial(kernel, groups, parts, width, bricks, scale),
-        out_shape=(
-            jax.ShapeDtypeStruct((width, bricks * VOX), bf16),
-            jax.ShapeDtypeStruct((width, bricks * VOX), bf16),
-            jax.ShapeDtypeStruct((rows_w, total), f32),
-        ),
-        in_specs=[smem, smem, smem, vmem, vmem, vmem],
-        out_specs=(vmem, vmem, vmem),
+        out_shape=outputs,
+        in_specs=[anywhere] * 6,
+        out_specs=(anywhere,) * 3,
         scratch_shapes=[
+            pltpu.SMEM((bricks, VOX // 32), jnp.int32),
+            pltpu.SMEM((bricks, 26), jnp.int32),
+            pltpu.SMEM((1, 8), jnp.int32),
+            pltpu.VMEM((width, bricks, VOX), bf16),
+            pltpu.VMEM((rows_w, total), bf16),
+            pltpu.VMEM((width, bricks, VOX), bf16),
+            pltpu.VMEM((width, bricks, VOX), bf16),
+            pltpu.VMEM((width, bricks, VOX), bf16),
+            pltpu.VMEM((rows_w, total), f32),
+            dma((6,)), dma((3,)),
             pltpu.VMEM((bricks + 9, TILES, width, LANES), bf16),
             pltpu.VMEM((8, TILES, width, LANES), bf16),
             pltpu.VMEM((9 * LANES, 2 * LANES), bf16),
@@ -454,9 +528,12 @@
             pltpu.VMEM((9 * width, 3 * total), bf16),
             pltpu.VMEM((width, bricks * cube), f32),
             pltpu.VMEM((rows_k, bricks * wide), bf16),
-            pltpu.VMEM((total, bricks * VOX), bf16),
-            pltpu.VMEM((parts, width, bricks * VOX), bf16),
-            pltpu.VMEM((total, bricks * VOX), bf16),
+            pltpu.VMEM((2, 2, width, bricks * VOX), bf16),
+            pltpu.VMEM((2, width, bricks * VOX), bf16),
+            pltpu.VMEM((2, width, bricks * VOX), bf16),
+            pltpu.VMEM((2, width, bricks * VOX), bf16),
+            pltpu.VMEM((2, width, bricks * VOX), bf16),
+            pltpu.VMEM((2, 2, width, bricks * VOX), bf16),
             pltpu.VMEM((3 * total, bricks * cube), bf16),
             pltpu.VMEM((9 * width, bricks * cube), f32),
             pltpu.VMEM((8, TILES, width, LANES), bf16),
@@ -466,18 +543,26 @@
             pltpu.VMEM((groups, chunk, total), bf16),
             pltpu.VMEM((owners * chunk, total), bf16),
             dma((8,)), dma((8,)), dma((8,)), dma((8,)),
-            dma((bricks, parts)), dma((bricks, parts)), dma((bricks, parts)), dma((bricks, parts)),
+            dma((bricks,)), dma((bricks,)), dma((bricks,)), dma((bricks,)),
+            dma((bricks,)), dma((bricks,)), dma((1,)), dma((1,)),
             dma((groups,)), dma((groups,)), dma((groups,)), dma((groups,)),
         ],
         compiler_params=pltpu.CompilerParams(
-            collective_id=0, has_side_effects=True, vmem_limit_bytes=40 * 2**20
+            collective_id=0, has_side_effects=True, vmem_limit_bytes=60 * 2**20
         ),
     )(
         mask_packed, neighbours, send_list.reshape(1, 8),
         features, weights.reshape(rows_w, total), cotangent,
     )
-    shape = (width, bricks, VOX)
-    return act.reshape(shape), grad_feat.reshape(shape), grad_w.reshape(27, width, total)
+    act, grad_feat, grad_w = pl.pallas_call(
+        hand_over,
+        out_shape=outputs,
+        in_specs=[anywhere] * 3,
+        out_specs=(anywhere,) * 3,
+        scratch_shapes=[dma((3,))],
+        compiler_params=pltpu.CompilerParams(vmem_limit_bytes=60 * 2**20),
+    )(*results)
+    return act, grad_feat, grad_w.reshape(27, width, total)
 
 
 def solution(mesh):

time: 40.2 us -> 53.6 us (1.33)
  Pallas kernels: 33.9 us -> 52.9 us
  local copies, waits for them, and re-layouts: 5.37 us -> 0 us
    pallas_call x0 -> x1, Pallas kernels: none -> 18.5 us  [on_device(): pl.pallas_call(hand_over, out_shape=outputs, in_specs=[anywhere] * 3, out...]
    unnamed x13 -> x0, local copies, waits for them, and re-layouts: 4.05 us -> none
    reshape x2 -> x0, local copies, waits for them, and re-layouts: 1.32 us -> none  [the longest x1 0.66 us: on_device(): act.reshape(shape)]
where the time goes in v3:
time: 53.6 us; the launch traced here: 53.5 us
  Pallas kernels  52.9 us (99%)
  between operations  0.64 us (1%)
    pallas_call x1, Pallas kernels, on_device(): pl.pallas_call(functools.partial(kernel, groups, parts, width, bricks, sc...  34.4 us
    pallas_call x1, Pallas kernels, on_device(): pl.pallas_call(hand_over, out_shape=outputs, in_specs=[anywhere] * 3, out...  18.5 us

profile of v3, /device:TPU:0, one launch (start us, length us, event | category | flops | bytes accessed | tf_op | source)
XLA Modules:
  0.0 53.5 jit_solution(18403819998044588664)
XLA Ops:
  0.6 34.4 %shard_map.85 = (bf16[32,2,512]{2,1,0:T(2,128)(2,1)}, bf16[32,2,512]{2,1,0:T(2,128)(2,1)}, f32[864,128]{1,0:T(8,128)}) custom-call(s32[2,16]{1,0:T(2,128)} %packed_in.1, s32[2,26]{1,0:T(2,128)} %near_in.1, s32[1,8]{1,0:T(1,128)} %bitcast.4, bf16[32,2,512]{2,1,0:T(2,128)(2,1)} %feat_in.1, bf16[864,128]{1,0:T(8,128)(2,1)} %bitcast.3, bf16[32,2,512]{2,1,0:T(2,128)(2,1)} %cot_in.1), custom_call_target="tpu_custom_call" | custom-call | tf_op jit(solution)/shard_map/pallas_call | solution.py:507
  35.0 18.5 %shard_map.86 = (bf16[32,2,512]{2,1,0:T(2,128)(2,1)}, bf16[32,2,512]{2,1,0:T(2,128)(2,1)}, f32[864,128]{1,0:T(8,128)}) custom-call(bf16[32,2,512]{2,1,0:T(2,128)(2,1)} %get-tuple-element.9.refs_0_, bf16[32,2,512]{2,1,0:T(2,128)(2,1)} %get-tuple-element.10.refs_1_, f32[864,128]{1,0:T(8,128)} %get-tuple-element.11.refs_2_), custom_call_target="tpu_custom_call" | custom-call | tf_op jit(solution)/shard_map/pallas_call | solution.py:557

commit v4 on v3

--- a/solution.py
+++ b/solution.py
@@ -48,10 +48,10 @@
 def kernel(
     groups, parts, width, bricks, scale,
     packed_in, near_in, sends_in, feat_in, w_in, cot_in,
-    act_out, grad_feat_out, grad_w_out,
-    packed, near, sends, feat, w, cot, act, grad_feat, grad_w, in_s, out_s,
+    act_out, grad_feat_out, gw_out,
+    packed, near, sends, feat, w, cot, act, grad_feat, gw_all, in_s, out_s,
     table, outbox, place, expand, w_turned, w_wide, padded, stacked, comp, mate_in, halves, cross_in, cots, gates,
-    window, prod, backbox, back_in, gw_own, gw_send, gw_in, gw_all,
+    window, prod, backbox, back_in, gw_own, gw_send, gw_in,
     halo_s, halo_r, back_s, back_r, mate_s, mate_r, cross_s, cross_r, gate_s, gate_r, cot_s, cot_r, red_s, red_r, all_s, all_r,
 ):
     me, mine = lax.axis_index("space"), lax.axis_index("chan")
@@ -83,85 +83,6 @@
         )
     for peer in (mate, across):
         pl.semaphore_signal(barrier, inc=1, device_id=(me, peer), device_id_type=MESH)
-    for fetch in fetches[:3]:
-        fetch.wait()
-
-    lane = lax.broadcasted_iota(jnp.int32, (1, VOX), 1)
-    masks = []
-    for b in range(bricks):
-        word = jnp.zeros((1, VOX), jnp.int32)
-        for i in range(VOX // 32):
-            word = jnp.where((lane >> 5) == i, packed[b, i], word)
-        masks.append((lax.shift_right_logical(word, lane & 31) & 1).astype(f32))
-
-    masked = [
-        feat[:, b, :].astype(f32) * masks[b] for b in range(bricks)
-    ]
-    for b in range(bricks):
-        for t in range(TILES):
-            table[b, t] = masked[b][:, t * LANES : (t + 1) * LANES].astype(bf16)
-    table[bricks + 8] = jnp.zeros((TILES, width, LANES), bf16)
-    for k, (a, _) in enumerate(tile_moves):
-        chosen = jnp.full((width, LANES), sends[0, k], jnp.int32)
-        for t in range(TILES) if a == 0 else (tile_of(a),):
-            value = jnp.zeros((width, LANES), f32)
-            for b in range(bricks):
-                value = jnp.where(chosen == b, masked[b][:, t * LANES : (t + 1) * LANES], value)
-            outbox[k, t] = value.astype(bf16)
-
-    pl.semaphore_wait(barrier, groups - 1 + 2)
-
-    tile_a, tile_b = me // 4, lax.rem(me, 4)
-
-    def inside(a, b):
-        return (
-            (tile_a + a >= 0) & (tile_a + a < groups // 4) & (tile_b + b >= 0) & (tile_b + b < 4)
-        )
-
-    def halo(k, box, rows, base, send, recv, sign):
-        a, _ = tile_moves[k]
-        if a == 0:
-            source, target = box.at[k], rows.at[base + k]
-        else:
-            source, target = box.at[k, tile_of(a)], rows.at[base + k, tile_of(a)]
-        peer = jnp.clip(me + sign * tile_steps[k], 0, groups - 1)
-        return pltpu.make_async_remote_copy(
-            src_ref=source, dst_ref=target, send_sem=send.at[k], recv_sem=recv.at[k],
-            device_id=(peer, mine), device_id_type=MESH,
-        )
-
-    forth = [halo(k, outbox, table, bricks, halo_s, halo_r, -1) for k in range(8)]
-    back = [halo(k, backbox, back_in, 0, back_s, back_r, 1) for k in range(8)]
-    ahead = [inside(a, b) for a, b in tile_moves]
-    behind = [inside(-a, -b) for a, b in tile_moves]
-
-    def start_if(flag, copy):
-        @pl.when(flag)
-        def _():
-            copy.start()
-
-    def sent_if(flag, copy):
-        @pl.when(flag)
-        def _():
-            copy.wait_send()
-
-    def arrived_if(flag, copy):
-        @pl.when(flag)
-        def _():
-            copy.wait_recv()
-
-    for k in range(8):
-        start_if(behind[k], forth[k])
-
-    for fetch in fetches[3:]:
-        fetch.wait()
-    for b in range(bricks):
-        cots[level, :, b * VOX : (b + 1) * VOX] = cot[:, b, :]
-    cot_copy = pltpu.make_async_remote_copy(
-        src_ref=cots.at[level], dst_ref=cots.at[level], send_sem=cot_s.at[0],
-        recv_sem=cot_r.at[0], device_id=(me, across), device_id_type=MESH,
-    )
-    cot_copy.start()
 
     row = lax.broadcasted_iota(jnp.int32, (LANES, 2 * LANES), 0)
     col = lax.broadcasted_iota(jnp.int32, (LANES, 2 * LANES), 1)
@@ -177,6 +98,86 @@
             hit = hit & side_z[z]
         place[n * LANES : (n + 1) * LANES, :] = jnp.where(hit, 1.0, 0.0).astype(bf16)
     expand[...] = jnp.where(col == goal - (PLANES + 1), 1.0, 0.0).astype(bf16)
+
+    for fetch in fetches[:3]:
+        fetch.wait()
+
+    lane = lax.broadcasted_iota(jnp.int32, (1, VOX), 1)
+    masks = []
+    for b in range(bricks):
+        word = jnp.zeros((1, VOX), jnp.int32)
+        for i in range(VOX // 32):
+            word = jnp.where((lane >> 5) == i, packed[b, i], word)
+        masks.append((lax.shift_right_logical(word, lane & 31) & 1).astype(f32))
+
+    masked = [
+        feat[:, b, :].astype(f32) * masks[b] for b in range(bricks)
+    ]
+    for b in range(bricks):
+        for t in range(TILES):
+            table[b, t] = masked[b][:, t * LANES : (t + 1) * LANES].astype(bf16)
+    table[bricks + 8] = jnp.zeros((TILES, width, LANES), bf16)
+    for k, (a, _) in enumerate(tile_moves):
+        chosen = jnp.full((width, LANES), sends[0, k], jnp.int32)
+        for t in range(TILES) if a == 0 else (tile_of(a),):
+            value = jnp.zeros((width, LANES), f32)
+            for b in range(bricks):
+                value = jnp.where(chosen == b, masked[b][:, t * LANES : (t + 1) * LANES], value)
+            outbox[k, t] = value.astype(bf16)
+
+    pl.semaphore_wait(barrier, groups - 1 + 2)
+
+    tile_a, tile_b = me // 4, lax.rem(me, 4)
+
+    def inside(a, b):
+        return (
+            (tile_a + a >= 0) & (tile_a + a < groups // 4) & (tile_b + b >= 0) & (tile_b + b < 4)
+        )
+
+    def halo(k, box, rows, base, send, recv, sign):
+        a, _ = tile_moves[k]
+        if a == 0:
+            source, target = box.at[k], rows.at[base + k]
+        else:
+            source, target = box.at[k, tile_of(a)], rows.at[base + k, tile_of(a)]
+        peer = jnp.clip(me + sign * tile_steps[k], 0, groups - 1)
+        return pltpu.make_async_remote_copy(
+            src_ref=source, dst_ref=target, send_sem=send.at[k], recv_sem=recv.at[k],
+            device_id=(peer, mine), device_id_type=MESH,
+        )
+
+    forth = [halo(k, outbox, table, bricks, halo_s, halo_r, -1) for k in range(8)]
+    back = [halo(k, backbox, back_in, 0, back_s, back_r, 1) for k in range(8)]
+    ahead = [inside(a, b) for a, b in tile_moves]
+    behind = [inside(-a, -b) for a, b in tile_moves]
+
+    def start_if(flag, copy):
+        @pl.when(flag)
+        def _():
+            copy.start()
+
+    def sent_if(flag, copy):
+        @pl.when(flag)
+        def _():
+            copy.wait_send()
+
+    def arrived_if(flag, copy):
+        @pl.when(flag)
+        def _():
+            copy.wait_recv()
+
+    for k in range(8):
+        start_if(behind[k], forth[k])
+
+    for fetch in fetches[3:]:
+        fetch.wait()
+    for b in range(bricks):
+        cots[level, :, b * VOX : (b + 1) * VOX] = cot[:, b, :]
+    cot_copy = pltpu.make_async_remote_copy(
+        src_ref=cots.at[level], dst_ref=cots.at[level], send_sem=cot_s.at[0],
+        recv_sem=cot_r.at[0], device_id=(me, across), device_id_type=MESH,
+    )
+    cot_copy.start()
 
     rows_k = w_turned.shape[1]
     for c in range(rows_k // LANES):
@@ -455,9 +456,8 @@
     for d in range(1, groups):
         source = lax.rem(me + groups - d, groups)
         guarded(source < owners, share_copy(d).wait_recv)
-    grad_w[...] = gw_all[0:rows_w, :].astype(f32)
-    w_copy = pltpu.make_async_copy(grad_w, grad_w_out, out_s.at[2])
-    w_copy.start()
+    gw_copy = pltpu.make_async_copy(gw_all, gw_out, out_s.at[2])
+    gw_copy.start()
 
     for k in range(8):
         sent_if(behind[k], forth[k])
@@ -473,18 +473,25 @@
         guarded(me < owners, share_copy(d).wait_send)
     act_copy.wait()
     feat_copy.wait()
-    w_copy.wait()
+    gw_copy.wait()
 
 
 def hand_over(*refs):
-    sources, targets, sem = refs[:3], refs[3:6], refs[6]
-    copies = [
-        pltpu.make_async_copy(sources[i], targets[i], sem.at[i]) for i in range(3)
+    sources, targets, held, wide, in_s, out_s = refs[:3], refs[3:6], refs[6:9], refs[9], *refs[10:]
+    fetches = [pltpu.make_async_copy(sources[i], held[i], in_s.at[i]) for i in range(3)]
+    stores = [
+        pltpu.make_async_copy(source, targets[i], out_s.at[i])
+        for i, source in enumerate((held[0], held[1], wide))
     ]
-    for copy in copies:
-        copy.start()
-    for copy in copies:
-        copy.wait()
+    for fetch in fetches:
+        fetch.start()
+    for i in range(3):
+        fetches[i].wait()
+        if i == 2:
+            wide[...] = held[2][0 : wide.shape[0], :].astype(jnp.float32)
+        stores[i].start()
+    for store in stores:
+        store.wait()
 
 
 def on_device(features, mask_packed, neighbours, send_list, weights, cotangent):
@@ -498,17 +505,14 @@
     scale = 1.0 / math.sqrt(bricks * groups * VOX)
     f32, bf16 = jnp.float32, jnp.bfloat16
     dma = pltpu.SemaphoreType.DMA
-    outputs = (
-        jax.ShapeDtypeStruct((width, bricks, VOX), bf16),
-        jax.ShapeDtypeStruct((width, bricks, VOX), bf16),
-        jax.ShapeDtypeStruct((rows_w, total), f32),
-    )
-    anywhere = pl.BlockSpec(memory_space=pl.ANY)
+    brick_shape = jax.ShapeDtypeStruct((width, bricks, VOX), bf16)
+    gw_shape = jax.ShapeDtypeStruct((owners * chunk, total), bf16)
+    hbm = pl.BlockSpec(memory_space=pl.ANY)
     results = pl.pallas_call(
         functools.partial(kernel, groups, parts, width, bricks, scale),
-        out_shape=outputs,
-        in_specs=[anywhere] * 6,
-        out_specs=(anywhere,) * 3,
+        out_shape=(brick_shape, brick_shape, gw_shape),
+        in_specs=[hbm] * 6,
+        out_specs=(hbm,) * 3,
         scratch_shapes=[
             pltpu.SMEM((bricks, VOX // 32), jnp.int32),
             pltpu.SMEM((bricks, 26), jnp.int32),
@@ -518,7 +522,7 @@
             pltpu.VMEM((width, bricks, VOX), bf16),
             pltpu.VMEM((width, bricks, VOX), bf16),
             pltpu.VMEM((width, bricks, VOX), bf16),
-            pltpu.VMEM((rows_w, total), f32),
+            pltpu.VMEM((owners * chunk, total), bf16),
             dma((6,)), dma((3,)),
             pltpu.VMEM((bricks + 9, TILES, width, LANES), bf16),
             pltpu.VMEM((8, TILES, width, LANES), bf16),
@@ -541,7 +545,6 @@
             pltpu.VMEM((owners * chunk, total), f32),
             pltpu.VMEM((owners * chunk, total), bf16),
             pltpu.VMEM((groups, chunk, total), bf16),
-            pltpu.VMEM((owners * chunk, total), bf16),
             dma((8,)), dma((8,)), dma((8,)), dma((8,)),
             dma((bricks,)), dma((bricks,)), dma((bricks,)), dma((bricks,)),
             dma((bricks,)), dma((bricks,)), dma((1,)), dma((1,)),
@@ -556,10 +559,18 @@
     )
     act, grad_feat, grad_w = pl.pallas_call(
         hand_over,
-        out_shape=outputs,
-        in_specs=[anywhere] * 3,
-        out_specs=(anywhere,) * 3,
-        scratch_shapes=[dma((3,))],
+        out_shape=(
+            brick_shape, brick_shape, jax.ShapeDtypeStruct((rows_w, total), f32)
+        ),
+        in_specs=[hbm] * 3,
+        out_specs=(hbm,) * 3,
+        scratch_shapes=[
+            pltpu.VMEM((width, bricks, VOX), bf16),
+            pltpu.VMEM((width, bricks, VOX), bf16),
+            pltpu.VMEM((owners * chunk, total), bf16),
+            pltpu.VMEM((rows_w, total), f32),
+            dma((3,)), dma((3,)),
+        ],
         compiler_params=pltpu.CompilerParams(vmem_limit_bytes=60 * 2**20),
     )(*results)
     return act, grad_feat, grad_w.reshape(27, width, total)

time: 53.6 us -> 36.9 us (0.69)
  Pallas kernels: 52.9 us -> 36.1 us
    pallas_call x1, Pallas kernels: 18.5 us -> 1.85 us  [on_device(): pl.pallas_call(hand_over, out_shape=(brick_shape, brick_shape, jax.ShapeD...]
where the time goes in v4:
time: 36.9 us; the launch traced here: 36.7 us
  Pallas kernels  36.1 us (98%)
  between operations  0.64 us (2%)
    pallas_call x1, Pallas kernels, on_device(): pl.pallas_call(functools.partial(kernel, groups, parts, width, bricks, sc...  34.2 us
    pallas_call x1, Pallas kernels, on_device(): pl.pallas_call(hand_over, out_shape=(brick_shape, brick_shape, jax.ShapeD...  1.85 us

profile of v4, /device:TPU:0, one launch (start us, length us, event | category | flops | bytes accessed | tf_op | source)
XLA Modules:
  0.0 36.7 jit_solution(14155097509725585877)
XLA Ops:
  0.6 34.2 %shard_map.85 = (bf16[32,2,512]{2,1,0:T(2,128)(2,1)}, bf16[32,2,512]{2,1,0:T(2,128)(2,1)}, bf16[896,128]{1,0:T(8,128)(2,1)}) custom-call(s32[2,16]{1,0:T(2,128)} %packed_in.1, s32[2,26]{1,0:T(2,128)} %near_in.1, s32[1,8]{1,0:T(1,128)} %bitcast.4, bf16[32,2,512]{2,1,0:T(2,128)(2,1)} %feat_in.1, bf16[864,128]{1,0:T(8,128)(2,1)} %bitcast.3, ...), custom_call_target="tpu_custom_call" | custom-call | tf_op jit(solution)/shard_map/pallas_call | solution.py:511
  34.9 1.9 %shard_map.86 = (bf16[32,2,512]{2,1,0:T(2,128)(2,1)}, bf16[32,2,512]{2,1,0:T(2,128)(2,1)}, f32[864,128]{1,0:T(8,128)}) custom-call(bf16[32,2,512]{2,1,0:T(2,128)(2,1)} %get-tuple-element.9.refs_0_, bf16[32,2,512]{2,1,0:T(2,128)(2,1)} %get-tuple-element.10.refs_1_, bf16[896,128]{1,0:T(8,128)(2,1)} %get-tuple-element.11.refs_2_), custom_call_target="tpu_custom_call" | custom-call | tf_op jit(solution)/shard_map/pallas_call | solution.py:560

commit v5 on v4

--- a/solution.py
+++ b/solution.py
@@ -300,11 +300,11 @@
                 cots[h, :, spans[b]].astype(f32) * masks[b] * gate * (1.0 + pre * (1.0 - gate))
             ).astype(bf16)
 
-            @pl.when(level == h)
-            def _():
-                act[:, b, :] = (pre * gate).astype(bf16)
-
         to_both[b].start()
+    for b in range(bricks):
+        pre = halves[level, :, spans[b]].astype(f32) + cross_in[level, :, spans[b]].astype(f32)
+        pre = pre * masks[b]
+        act[:, b, :] = (pre * jax.nn.sigmoid(pre)).astype(bf16)
     act_copy = pltpu.make_async_copy(act, act_out, out_s.at[0])
     act_copy.start()
 
@@ -332,12 +332,25 @@
 
     kept_me = jnp.minimum(me, owners - 1)
 
-    def share_copy(d):
-        peer = lax.rem(me + d, groups)
+    partner = me + 1 - 2 * lax.rem(me, 2)
+    pairs = groups // 2
+
+    def share_copy(k):
         span = gw_all.at[chunk_rows(kept_me)]
+        peer = partner if k == 0 else lax.rem(me + 2 * k, groups)
         return pltpu.make_async_remote_copy(
-            src_ref=span, dst_ref=span, send_sem=all_s.at[d], recv_sem=all_r.at[d],
+            src_ref=span, dst_ref=span, send_sem=all_s.at[k], recv_sem=all_r.at[k],
             device_id=(peer, mine), device_id_type=MESH,
+        )
+
+    def source_of(device, k):
+        return lax.rem(device + groups - 2 * k, groups)
+
+    def forward_copy(k):
+        span = gw_all.at[chunk_rows(jnp.minimum(source_of(me, k), owners - 1))]
+        return pltpu.make_async_remote_copy(
+            src_ref=span, dst_ref=span, send_sem=all_s.at[pairs + k],
+            recv_sem=all_r.at[pairs + k], device_id=(partner, mine), device_id_type=MESH,
         )
 
     def guarded(flag, action):
@@ -374,6 +387,17 @@
     for n in range(1, 9):
         spread = spread + pltpu.roll(prod[n * width : (n + 1) * width, :], shifts[n], axis=1)
     padded[...] = spread
+
+    def add_up():
+        value = gw_own[chunk_rows(kept_me), :]
+        for d in range(1, groups):
+            reduce_copy(d)[1].wait_recv()
+            value = value + gw_in[d].astype(f32)
+        gw_all[chunk_rows(kept_me), :] = (value * scale).astype(bf16)
+        for k in range(pairs):
+            share_copy((k + 1) % pairs).start()
+
+    guarded(me < owners, add_up)
 
     pieces = []
     blank = jnp.zeros((width, LANES), f32)
@@ -425,16 +449,10 @@
             backbox[k, tile_of(a)] = slots[k].astype(bf16)
         start_if(ahead[k], back[k])
 
-    def add_up():
-        value = gw_own[chunk_rows(kept_me), :]
-        for d in range(1, groups):
-            reduce_copy(d)[1].wait_recv()
-            value = value + gw_in[d].astype(f32)
-        gw_all[chunk_rows(kept_me), :] = (value * scale).astype(bf16)
-        for d in range(1, groups):
-            share_copy(d).start()
-
-    guarded(me < owners, add_up)
+    for k in range(1, pairs):
+        flag = source_of(me, k) < owners
+        guarded(flag, share_copy(k).wait_recv)
+        guarded(flag, forward_copy(k).start)
 
     for k in range(8):
         arrived_if(behind[k], back[k])
@@ -453,9 +471,9 @@
     feat_copy = pltpu.make_async_copy(grad_feat, grad_feat_out, out_s.at[1])
     feat_copy.start()
 
-    for d in range(1, groups):
-        source = lax.rem(me + groups - d, groups)
-        guarded(source < owners, share_copy(d).wait_recv)
+    guarded(partner < owners, share_copy(0).wait_recv)
+    for k in range(1, pairs):
+        guarded(source_of(partner, k) < owners, forward_copy(k).wait_recv)
     gw_copy = pltpu.make_async_copy(gw_all, gw_out, out_s.at[2])
     gw_copy.start()
 
@@ -470,7 +488,10 @@
     for d in range(1, groups):
         peer, copy = reduce_copy(d)
         guarded(peer < owners, copy.wait_send)
-        guarded(me < owners, share_copy(d).wait_send)
+    for k in range(pairs):
+        guarded(me < owners, share_copy(k).wait_send)
+        if k:
+            guarded(source_of(me, k) < owners, forward_copy(k).wait_send)
     act_copy.wait()
     feat_copy.wait()
     gw_copy.wait()

time: 36.9 us -> 38.7 us (1.049)
  Pallas kernels: 36.1 us -> 37.9 us
    pallas_call x1, Pallas kernels: 34.2 us -> 36.1 us  [on_device(): pl.pallas_call(functools.partial(kernel, groups, parts, width, bricks, sc...]
where the time goes in v5:
time: 38.7 us; the launch traced here: 38.6 us
  Pallas kernels  37.9 us (98%)
  between operations  0.64 us (2%)
    pallas_call x1, Pallas kernels, on_device(): pl.pallas_call(functools.partial(kernel, groups, parts, width, bricks, sc...  36.1 us
    pallas_call x1, Pallas kernels, on_device(): pl.pallas_call(hand_over, out_shape=(brick_shape, brick_shape, jax.ShapeD...  1.85 us

profile of v5, /device:TPU:0, one launch (start us, length us, event | category | flops | bytes accessed | tf_op | source)
XLA Modules:
  0.0 38.6 jit_solution(15530982675702348132)
XLA Ops:
  0.6 36.1 %shard_map.85 = (bf16[32,2,512]{2,1,0:T(2,128)(2,1)}, bf16[32,2,512]{2,1,0:T(2,128)(2,1)}, bf16[896,128]{1,0:T(8,128)(2,1)}) custom-call(s32[2,16]{1,0:T(2,128)} %packed_in.1, s32[2,26]{1,0:T(2,128)} %near_in.1, s32[1,8]{1,0:T(1,128)} %bitcast.4, bf16[32,2,512]{2,1,0:T(2,128)(2,1)} %feat_in.1, bf16[864,128]{1,0:T(8,128)(2,1)} %bitcast.3, ...), custom_call_target="tpu_custom_call" | custom-call | tf_op jit(solution)/shard_map/pallas_call | solution.py:532
  36.7 1.9 %shard_map.86 = (bf16[32,2,512]{2,1,0:T(2,128)(2,1)}, bf16[32,2,512]{2,1,0:T(2,128)(2,1)}, f32[864,128]{1,0:T(8,128)}) custom-call(bf16[32,2,512]{2,1,0:T(2,128)(2,1)} %get-tuple-element.9.refs_0_, bf16[32,2,512]{2,1,0:T(2,128)(2,1)} %get-tuple-element.10.refs_1_, bf16[896,128]{1,0:T(8,128)(2,1)} %get-tuple-element.11.refs_2_), custom_call_target="tpu_custom_call" | custom-call | tf_op jit(solution)/shard_map/pallas_call | solution.py:581

commit v6 on v4

--- a/solution.py
+++ b/solution.py
@@ -50,7 +50,7 @@
     packed_in, near_in, sends_in, feat_in, w_in, cot_in,
     act_out, grad_feat_out, gw_out,
     packed, near, sends, feat, w, cot, act, grad_feat, gw_all, in_s, out_s,
-    table, outbox, place, expand, w_turned, w_wide, padded, stacked, comp, mate_in, halves, cross_in, cots, gates,
+    table, outbox, place, expand, fold, compact, rimmed, w_turned, w_wide, padded, stacked, comp, mate_in, halves, cross_in, cots, gates,
     window, prod, backbox, back_in, gw_own, gw_send, gw_in,
     halo_s, halo_r, back_s, back_r, mate_s, mate_r, cross_s, cross_r, gate_s, gate_r, cot_s, cot_r, red_s, red_r, all_s, all_r,
 ):
@@ -97,6 +97,10 @@
         if z != 0:
             hit = hit & side_z[z]
         place[n * LANES : (n + 1) * LANES, :] = jnp.where(hit, 1.0, 0.0).astype(bf16)
+    row_t = lax.broadcasted_iota(jnp.int32, (2 * LANES, LANES), 0)
+    col_t = lax.broadcasted_iota(jnp.int32, (2 * LANES, LANES), 1)
+    goal_t = (col_t >> 6) * LANES + (((col_t >> 3) & 7) + 1) * PLANES + ((col_t & 7) + 1)
+    compact[...] = jnp.where(row_t == goal_t - (PLANES + 1), 1.0, 0.0).astype(bf16)
     expand[...] = jnp.where(col == goal - (PLANES + 1), 1.0, 0.0).astype(bf16)
 
     for fetch in fetches[:3]:
@@ -186,22 +190,8 @@
         if have < LANES:
             block = jnp.concatenate([block, jnp.zeros((LANES - have, total), f32)], axis=0)
         w_turned[:, c * LANES : (c + 1) * LANES] = block.T.astype(bf16)
-    for n in range(9):
-        for u in range(3):
-            w_wide[n * width : (n + 1) * width, u * total : (u + 1) * total] = w[
-                (u * 9 + n) * width : (u * 9 + n + 1) * width, :
-            ]
     if rows_k > rows_w:
         stacked[rows_w:, :] = jnp.zeros((rows_k - rows_w, bricks * wide), bf16)
-    for u in range(3):
-        for b in range(bricks):
-            for px in range(PLANES):
-                if not u <= px < u + BRICK:
-                    window[
-                        u * total : (u + 1) * total,
-                        b * cube + px * LANES : b * cube + (px + 1) * LANES,
-                    ] = jnp.zeros((total, LANES), bf16)
-
     for k in range(8):
         arrived_if(ahead[k], forth[k])
 
@@ -215,27 +205,26 @@
             for b in range(bricks):
                 pieces.append(table[near[b, neighbour_slot(x, y, z)], tile_of(x)])
         columns.append(jnp.concatenate(pieces, axis=0))
-    built = nn_dot(jnp.concatenate(columns, axis=1), place[...])
+    built = nn_dot(jnp.concatenate(columns, axis=1), place[...]).astype(bf16)
     ends = bricks * TILES * width
     for b in range(bricks):
         base = b * cube
         first = ends + b * width
         last = ends + (bricks + b) * width
-        padded[:, base : base + LANES] = built[first : first + width, LANES:]
-        padded[:, base + cube - LANES : base + cube] = built[last : last + width, :LANES]
+        rimmed[:, base : base + LANES] = built[first : first + width, LANES:]
+        rimmed[:, base + cube - LANES : base + cube] = built[last : last + width, :LANES]
         for t in range(TILES):
             at = (b * TILES + t) * width
-            padded[:, base + (2 * t + 1) * LANES : base + (2 * t + 3) * LANES] = built[
+            rimmed[:, base + (2 * t + 1) * LANES : base + (2 * t + 3) * LANES] = built[
                 at : at + width, :
             ]
 
     length = bricks * cube
     shifts = [(y + 1) * PLANES + (z + 1) for y, z in plane_offsets]
     for n in range(9):
-        value = padded[...]
+        value = rimmed[...]
         if shifts[n]:
             value = pltpu.roll(value, length - shifts[n], axis=1)
-        value = value.astype(bf16)
         for u in range(3):
             for b in range(bricks):
                 stacked[
@@ -276,7 +265,7 @@
             i = b * TILES + t
             part = nn_dot(w_turned[...], stacked[:, 2 * i * LANES : 2 * (i + 1) * LANES])
             comp[:, :, :, i * LANES : (i + 1) * LANES] = (
-                nt_dot(part.astype(bf16), expand[...])
+                nn_dot(part.astype(bf16), compact[...])
                 .astype(bf16)
                 .reshape(2, 2, width, LANES)
             )
@@ -288,6 +277,28 @@
             comp[:, low, :, spans[b]].astype(f32) + mate_in[:, :, spans[b]].astype(f32)
         ).astype(bf16)
         to_across[b].start()
+
+    for n in range(9):
+        for u in range(3):
+            w_wide[n * width : (n + 1) * width, u * total : (u + 1) * total] = w[
+                (u * 9 + n) * width : (u * 9 + n + 1) * width, :
+            ]
+    for u in range(3):
+        for b in range(bricks):
+            for px in range(PLANES):
+                if not u <= px < u + BRICK:
+                    window[
+                        u * total : (u + 1) * total,
+                        b * cube + px * LANES : b * cube + (px + 1) * LANES,
+                    ] = jnp.zeros((total, LANES), bf16)
+
+    for n, (y, z) in enumerate(plane_offsets):
+        hit = row_t == goal_t + (BRICK * PLANES * y + BRICK * z)
+        if y != 0:
+            hit = hit & ((col_t >> 3) & 7 == (BRICK - 1 if y == -1 else 0))
+        if z != 0:
+            hit = hit & (col_t & 7 == (BRICK - 1 if z == -1 else 0))
+        fold[:, n * LANES : (n + 1) * LANES] = jnp.where(hit, 1.0, 0.0).astype(bf16)
 
     cot_copy.wait_recv()
     for b in range(bricks):
@@ -300,11 +311,11 @@
                 cots[h, :, spans[b]].astype(f32) * masks[b] * gate * (1.0 + pre * (1.0 - gate))
             ).astype(bf16)
 
-            @pl.when(level == h)
-            def _():
-                act[:, b, :] = (pre * gate).astype(bf16)
-
         to_both[b].start()
+    for b in range(bricks):
+        pre = halves[level, :, spans[b]].astype(f32) + cross_in[level, :, spans[b]].astype(f32)
+        pre = pre * masks[b]
+        act[:, b, :] = (pre * jax.nn.sigmoid(pre)).astype(bf16)
     act_copy = pltpu.make_async_copy(act, act_out, out_s.at[0])
     act_copy.start()
 
@@ -393,11 +404,14 @@
     own_end = {(b, x): blank for b in range(bricks) for x in (-1, 1)}
     slots = [jnp.zeros((whole if a == 0 else width, LANES), f32) for a, _ in tile_moves]
 
+    def weighed(index, wanted, value):
+        return value * jnp.where(index == wanted, 1.0, 0.0).astype(f32)
+
     def picked(index, wanted, value):
         return jnp.where(jnp.full(value.shape, index, jnp.int32) == wanted, value, 0.0)
 
     for n, (y, z) in enumerate(plane_offsets):
-        folded = nt_dot(rims, place[n * LANES : (n + 1) * LANES, :])
+        folded = nn_dot(rims, fold[:, n * LANES : (n + 1) * LANES])
         for x in (-1, 0, 1):
             slot = None if (x, y) == (0, 0) else tile_moves.index((x, y))
             for b in range(bricks):
@@ -411,13 +425,13 @@
                     continue
                 index = near[b, neighbour_slot(x, y, z)]
                 for c in range(bricks):
-                    term = picked(index, c, piece)
+                    term = weighed(index, c, piece)
                     if x == 0:
                         own[c] = own[c] + term
                     else:
                         own_end[c, x] = own_end[c, x] + term
                 if slot is not None:
-                    slots[slot] = slots[slot] + picked(index, bricks + slot, piece)
+                    slots[slot] = slots[slot] + weighed(index, bricks + slot, piece)
     for k, (a, _) in enumerate(tile_moves):
         if a == 0:
             backbox[k] = slots[k].astype(bf16).reshape(TILES, width, LANES)
@@ -528,6 +542,9 @@
             pltpu.VMEM((8, TILES, width, LANES), bf16),
             pltpu.VMEM((9 * LANES, 2 * LANES), bf16),
             pltpu.VMEM((LANES, 2 * LANES), bf16),
+            pltpu.VMEM((2 * LANES, 9 * LANES), bf16),
+            pltpu.VMEM((2 * LANES, LANES), bf16),
+            pltpu.VMEM((width, bricks * cube), bf16),
             pltpu.VMEM((total, rows_k), bf16),
             pltpu.VMEM((9 * width, 3 * total), bf16),
             pltpu.VMEM((width, bricks * cube), f32),

time: 36.9 us -> 36.8 us (level)
  no operation moved by 1% of the time
where the time goes in v6:
time: 36.8 us; the launch traced here: 36.7 us
  Pallas kernels  36 us (98%)
  between operations  0.64 us (2%)
    pallas_call x1, Pallas kernels, on_device(): pl.pallas_call(functools.partial(kernel, groups, parts, width, bricks, sc...  34.2 us
    pallas_call x1, Pallas kernels, on_device(): pl.pallas_call(hand_over, out_shape=(brick_shape, brick_shape, jax.ShapeD...  1.85 us

profile of v6, /device:TPU:0, one launch (start us, length us, event | category | flops | bytes accessed | tf_op | source)
XLA Modules:
  0.0 36.7 jit_solution(16596639236912059145)
XLA Ops:
  0.6 34.2 %shard_map.85 = (bf16[32,2,512]{2,1,0:T(2,128)(2,1)}, bf16[32,2,512]{2,1,0:T(2,128)(2,1)}, bf16[896,128]{1,0:T(8,128)(2,1)}) custom-call(s32[2,16]{1,0:T(2,128)} %packed_in.1, s32[2,26]{1,0:T(2,128)} %near_in.1, s32[1,8]{1,0:T(1,128)} %bitcast.4, bf16[32,2,512]{2,1,0:T(2,128)(2,1)} %feat_in.1, bf16[864,128]{1,0:T(8,128)(2,1)} %bitcast.3, ...), custom_call_target="tpu_custom_call" | custom-call | tf_op jit(solution)/shard_map/pallas_call | solution.py:525
  34.8 1.9 %shard_map.86 = (bf16[32,2,512]{2,1,0:T(2,128)(2,1)}, bf16[32,2,512]{2,1,0:T(2,128)(2,1)}, f32[864,128]{1,0:T(8,128)}) custom-call(bf16[32,2,512]{2,1,0:T(2,128)(2,1)} %get-tuple-element.9.refs_0_, bf16[32,2,512]{2,1,0:T(2,128)(2,1)} %get-tuple-element.10.refs_1_, bf16[896,128]{1,0:T(8,128)(2,1)} %get-tuple-element.11.refs_2_), custom_call_target="tpu_custom_call" | custom-call | tf_op jit(solution)/shard_map/pallas_call | solution.py:577

commit v7 on v6

--- a/solution.py
+++ b/solution.py
@@ -385,6 +385,17 @@
     for n in range(1, 9):
         spread = spread + pltpu.roll(prod[n * width : (n + 1) * width, :], shifts[n], axis=1)
     padded[...] = spread
+
+    def add_up():
+        value = gw_own[chunk_rows(kept_me), :]
+        for d in range(1, groups):
+            reduce_copy(d)[1].wait_recv()
+            value = value + gw_in[d].astype(f32)
+        gw_all[chunk_rows(kept_me), :] = (value * scale).astype(bf16)
+        for d in range(1, groups):
+            share_copy(d).start()
+
+    guarded(me < owners, add_up)
 
     pieces = []
     blank = jnp.zeros((width, LANES), f32)
@@ -438,17 +449,6 @@
         else:
             backbox[k, tile_of(a)] = slots[k].astype(bf16)
         start_if(ahead[k], back[k])
-
-    def add_up():
-        value = gw_own[chunk_rows(kept_me), :]
-        for d in range(1, groups):
-            reduce_copy(d)[1].wait_recv()
-            value = value + gw_in[d].astype(f32)
-        gw_all[chunk_rows(kept_me), :] = (value * scale).astype(bf16)
-        for d in range(1, groups):
-            share_copy(d).start()
-
-    guarded(me < owners, add_up)
 
     for k in range(8):
         arrived_if(behind[k], back[k])

time: 36.8 us -> 38.4 us (1.043)
  Pallas kernels: 36 us -> 37.6 us
    pallas_call x1, Pallas kernels: 34.2 us -> 35.7 us  [on_device(): pl.pallas_call(functools.partial(kernel, groups, parts, width, bricks, sc...]
where the time goes in v7:
time: 38.4 us; the launch traced here: 38.2 us
  Pallas kernels  37.6 us (98%)
  between operations  0.64 us (2%)
    pallas_call x1, Pallas kernels, on_device(): pl.pallas_call(functools.partial(kernel, groups, parts, width, bricks, sc...  35.7 us
    pallas_call x1, Pallas kernels, on_device(): pl.pallas_call(hand_over, out_shape=(brick_shape, brick_shape, jax.ShapeD...  1.85 us

profile of v7, /device:TPU:0, one launch (start us, length us, event | category | flops | bytes accessed | tf_op | source)
XLA Modules:
  0.0 38.2 jit_solution(6671676773784670618)
XLA Ops:
  0.6 35.7 %shard_map.85 = (bf16[32,2,512]{2,1,0:T(2,128)(2,1)}, bf16[32,2,512]{2,1,0:T(2,128)(2,1)}, bf16[896,128]{1,0:T(8,128)(2,1)}) custom-call(s32[2,16]{1,0:T(2,128)} %packed_in.1, s32[2,26]{1,0:T(2,128)} %near_in.1, s32[1,8]{1,0:T(1,128)} %bitcast.4, bf16[32,2,512]{2,1,0:T(2,128)(2,1)} %feat_in.1, bf16[864,128]{1,0:T(8,128)(2,1)} %bitcast.3, ...), custom_call_target="tpu_custom_call" | custom-call | tf_op jit(solution)/shard_map/pallas_call | solution.py:525
  36.4 1.9 %shard_map.86 = (bf16[32,2,512]{2,1,0:T(2,128)(2,1)}, bf16[32,2,512]{2,1,0:T(2,128)(2,1)}, f32[864,128]{1,0:T(8,128)}) custom-call(bf16[32,2,512]{2,1,0:T(2,128)(2,1)} %get-tuple-element.9.refs_0_, bf16[32,2,512]{2,1,0:T(2,128)(2,1)} %get-tuple-element.10.refs_1_, bf16[896,128]{1,0:T(8,128)(2,1)} %get-tuple-element.11.refs_2_), custom_call_target="tpu_custom_call" | custom-call | tf_op jit(solution)/shard_map/pallas_call | solution.py:577
